TPU v7x, 128 devices: a whole 4x4x4 slice. The times are simulated.
128 devices in a mesh: row: 4 (over x), col: 32 (over y, z, core).
Axes of the slice: x: 4, y: 4, z: 4, core: 2. Of those that a mesh axis runs over, the one named last changes fastest.
Arguments:
- front: float32 [8, 4, 256, 1, 32, 256], P(None, 'row', None, None, 'col'), as said below
- child_tiles: float32 [4, 32, 32, 256, 256], P('row', 'col'), may hold values from -0.875 to 0.875
- child_owner: int32 [4, 32, 32], P('row', 'col'), may hold values from 0 to 31, each once within a row
- child_place: int32 [4, 32, 32], P('row', 'col'), may hold values from 0 to 7
- child_count: int32 [4, 32], P('row', 'col'), may hold values from 24 to 32, as said below
- tile_mask: int32 [32], replicated, may hold values from 0 to 1, as said below
Outputs:
- factored: float32 [8, 4, 256, 1, 32, 256], P(None, 'row', None, None, 'col')
Inputs may be any that keep to these rules, and one draw needn't show every extreme that they name: `child_owner`: each device names every column device exactly once among its 32 slots. `child_count`: some device has all 32 slots live. `front`: symmetric positive definite; its leading 2 * 512 rows and columns stay positive definite after the children are added. `tile_mask`: among the tile rows below all panels, some entry is 0 and some is 1.
All inputs are finite; a program needn't handle non-finite values.
Results may differ from a plain program's by a relative error of at most 0.0001.
Values sent between devices are 32-bit elements; how exact they have to be, the bound alone decides.
A program may use at most 128 MiB of HBM per device.

v0:
```python
import jax
import jax.numpy as jnp
from jax import lax
from jax.sharding import PartitionSpec as P

PANEL = 512
NPANEL = 2


def broadcast(block, axis, owner):
    block = jnp.where(lax.axis_index(axis) == owner, block, jnp.zeros_like(block))
    return lax.psum(block, axis)


def local(front, child_tiles, child_owner, child_place, child_count, tile_mask):
    n_row = lax.axis_size("row")
    n_col = lax.axis_size("col")
    row_id = lax.axis_index("row")
    col_id = lax.axis_index("col")
    rows_t = front.shape[0]
    cols_t = front.shape[3]
    tile = front.shape[2]
    highest = lax.Precision.HIGHEST
    blocks = front.reshape(rows_t, tile, cols_t, tile).transpose(0, 2, 1, 3)
    slots = child_tiles.shape[2]
    owner = child_owner.reshape(slots)
    place = child_place.reshape(slots)
    count = child_count.reshape(())
    order_ids = jnp.arange(slots, dtype=jnp.int32)
    valid = order_ids < count
    select = (
        (jnp.arange(n_col, dtype=jnp.int32)[:, None] == owner[None, :]) & valid[None, :]
    ).astype(jnp.float32)
    payload = jnp.einsum(
        "qs,sef->qef", select, child_tiles.reshape(slots, tile, tile), precision=highest
    )
    labels = jnp.dot(select, (place + 1).astype(jnp.float32), precision=highest)
    got_tiles, got_labels = (
        lax.all_to_all(payload, "col", split_axis=0, concat_axis=0, tiled=True),
        lax.all_to_all(labels, "col", split_axis=0, concat_axis=0, tiled=True),
    )
    local_count = rows_t * cols_t
    wanted = (jnp.arange(local_count, dtype=jnp.int32) + 1).astype(jnp.float32)
    placing = (got_labels[None, :] == wanted[:, None]).astype(jnp.float32)
    added = jnp.einsum("tq,qef->tef", placing, got_tiles, precision=highest)
    blocks = blocks + added.reshape(rows_t, cols_t, tile, tile)
    row_tiles = jnp.arange(rows_t, dtype=jnp.int32) * n_row + row_id
    col_tiles = jnp.arange(cols_t, dtype=jnp.int32) * n_col + col_id
    all_tiles = jnp.arange(tile_mask.shape[0], dtype=jnp.int32)
    mask_rows = jnp.sum(
        (row_tiles[:, None] == all_tiles[None, :]).astype(jnp.int32) * tile_mask[None, :], axis=1
    )
    ident = jnp.eye(PANEL, dtype=jnp.float32)
    home = jnp.arange(cols_t, dtype=jnp.int32) * (n_col // n_row) + col_id // n_row
    per_panel = PANEL // tile
    panel_tiles = NPANEL * per_panel
    for step in range(NPANEL):
        first = step * per_panel
        column = blocks[:, 0]
        left = broadcast(column, "col", first)
        right = broadcast(column, "col", first + 1)
        panel = jnp.concatenate([left, right], axis=2)
        lead = first // n_row
        near = lax.all_gather(panel[lead], "row", axis=0, tiled=True)
        offset = first % n_row * tile
        diagonal = near[offset : offset + PANEL]
        factor = jnp.linalg.cholesky(diagonal)
        inverse = jax.scipy.linalg.solve_triangular(factor, ident, lower=True)
        kept_rows = (mask_rows == 1) | (row_tiles < panel_tiles)
        keep = ((row_tiles >= first + per_panel) & kept_rows).astype(jnp.float32)
        masked = panel * keep[:, None, None]
        lower = jnp.dot(masked.reshape(rows_t * tile, PANEL), inverse.T, precision=highest)
        lower = lower.reshape(rows_t, tile, PANEL)
        chosen = jnp.take(lower, home, axis=0)
        across = broadcast(chosen, "row", col_id % n_row)
        blocks = blocks - jnp.einsum("aep,bfp->abef", lower, across, precision=highest)
        is_first = (row_tiles == first).astype(jnp.float32)[:, None, None]
        is_second = (row_tiles == first + 1).astype(jnp.float32)[:, None, None]
        fresh = lower + is_first * factor[None, :tile, :] + is_second * factor[None, tile:, :]
        new_column = jnp.where(
            col_id == first,
            fresh[:, :, :tile],
            jnp.where(col_id == first + 1, fresh[:, :, tile:], blocks[:, 0]),
        )
        blocks = blocks.at[:, 0].set(new_column)
        row_sel = (row_tiles == first) | (row_tiles == first + 1)
        col_sel = col_tiles >= first + per_panel
        blocks = jnp.where(row_sel[:, None, None, None] & col_sel[None, :, None, None], 0.0, blocks)
    return blocks.transpose(0, 2, 1, 3).reshape(rows_t, 1, tile, cols_t, 1, tile)


def solution(mesh):
    return jax.shard_map(
        local,
        mesh=mesh,
        in_specs=(
            P(None, "row", None, None, "col", None),
            P("row", "col", None, None, None),
            P("row", "col", None),
            P("row", "col", None),
            P("row", "col"),
            P(),
        ),
        out_specs=P(None, "row", None, None, "col", None),
        check_vma=False,
    )
```

profile of v0, /device:TPU:48, one launch (start us, length us, event | category | flops | bytes accessed | tf_op | source)
XLA Modules:
  0.0 940.1 jit_solution(17132413544090728176)
XLA Ops:
  8.6 8.0 all-to-all-start
  16.6 12.5 %fusion.2 = f32[32,256,256]{2,0,1:T(8,128)S(1)} fusion(f32[32,256,256]{2,1,0:T(8,128)} %bitcast.184, s32[32]{0:T(128)} %bitcast.186, pred[32]{0:T(512)(128)(4,1)S(1)} %iota_compare_fusion.6), kind=kOutput, calls=%fused_computation.6 | convolution fusion | flops 805308416 | bytes 16777376 | tf_op jit(solution)/shard_map/qs,sef->qef/dot_general | solution.py:34
  29.1 8.1 copy.55
  37.2 7.4 all-to-all-start.1
  44.8 4.6 copy.52
  49.7 119.0 %all-to-all-done.1 = f32[32,256,256]{2,1,0:T(8,128)} async-done(((f32[32,256,256]{2,1,0:T(8,128)}), f32[32,256,256]{2,1,0:T(8,128)}, u32[]{:S(2)}, u32[]{:S(2)}) %all-to-all-start.1) | async-done | bytes 8388640 | tf_op jit(solution)/shard_map/all_to_all | solution.py:39
  168.7 11.8 %fusion = f32[8,256,256]{2,0,1:T(8,128)} fusion(f32[32,256,256]{2,1,0:T(8,128)} %all-to-all-done.1, f32[32]{0:T(128)S(1)} %reduce.20, f32[8]{0:T(128)S(1)} %add_convert_fusion), kind=kOutput, calls=%fused_computation.4 | convolution fusion | flops 201326848 | bytes 10485920 | tf_op jit(solution)/shard_map/tq,qef->tef/dot_general | solution.py:45
  180.5 3.0 copy.57
  183.4 4.0 broadcast_select_fusion.2
  187.5 110.5 %all-reduce.14.cloned.1.call-done = (f32[8,256,256]{1,2,0:T(8,128)}, f32[8,256,256]{1,2,0:T(8,128)}) async-done(((f32[8,256,256]{1,2,0:T(8,128)}, f32[8,256,256]{1,2,0:T(8,128)}), (f32[8,256,256]{1,2,0:T(8,128)}, f32[8,256,256]{1,2,0:T(8,128)})) %all-reduce.14.cloned.1.call-update) | async-done | bytes 4194320 | tf_op jit(solution)/shard_map/psum | solution.py:12
  298.0 1.9 constant_dynamic-update-slice_fusion.1
  300.4 1.9 copy-done.2
  303.9 31.1 %all-gather.5.cloned.1.call-done = f32[1,1024,512]{1,2,0:T(8,128)} async-done(((f32[1,256,512]{1,2,0:T(8,128)}), f32[1,1024,512]{1,2,0:T(8,128)}) %all-gather.5.cloned.1.call-update) | async-done | bytes 2097168 | tf_op jit(solution)/shard_map/all_gather | solution.py:64
  335.0 2.3 slice_bitcast_fusion.1
  337.3 2.6 copy.58
  339.8 1.8 fusion.30
  342.6 11.7 %cholesky.286 = f32[128,128]{1,0:T(8,128)S(1)} custom-call(f32[128,128]{1,0:T(8,128)S(1)} %cholesky.426), custom_call_target="Cholesky" | custom-call | tf_op jit(solution)/shard_map/jit(cholesky)/cholesky | solution.py:67
  355.4 9.8 %custom-call.27 = f32[1,128,128]{1,2,0:T(8,128)S(1)} custom-call(f32[1,128,128]{2,1,0:T(8,128)S(1)} %get-tuple-element.114), custom_call_target="InvertDiagBlocksLowerTriangular" | custom-call | tf_op jit(solution)/shard_map/jit(cholesky)/cholesky | solution.py:67
  365.2 1.9 constant_dynamic-update-slice_fusion.9
  368.4 11.7 %cholesky.305 = f32[128,128]{1,0:T(8,128)S(1)} custom-call(f32[128,128]{1,0:T(8,128)S(1)} %cholesky.430), custom_call_target="Cholesky" | custom-call | tf_op jit(solution)/shard_map/jit(cholesky)/cholesky | solution.py:67
  380.8 10.2 %custom-call.28 = f32[1,128,128]{1,2,0:T(8,128)S(1)} custom-call(f32[1,128,128]{2,1,0:T(8,128)S(1)} %get-tuple-element.111), custom_call_target="InvertDiagBlocksLowerTriangular" | custom-call | tf_op jit(solution)/shard_map/jit(cholesky)/cholesky | solution.py:67
  393.4 11.7 %cholesky.326 = f32[128,128]{1,0:T(8,128)S(1)} custom-call(f32[128,128]{1,0:T(8,128)S(1)} %cholesky.435), custom_call_target="Cholesky" | custom-call | tf_op jit(solution)/shard_map/jit(cholesky)/cholesky | solution.py:67
  406.4 9.8 %custom-call.29 = f32[1,128,128]{1,2,0:T(8,128)S(1)} custom-call(f32[1,128,128]{2,1,0:T(8,128)S(1)} %get-tuple-element.108), custom_call_target="InvertDiagBlocksLowerTriangular" | custom-call | tf_op jit(solution)/shard_map/jit(cholesky)/cholesky | solution.py:67
  418.5 11.9 %cholesky.343 = f32[128,128]{1,0:T(8,128)S(1)} custom-call(f32[128,128]{1,0:T(8,128)S(1)} %convolution_subtract_fusion.11), custom_call_target="Cholesky" | custom-call | tf_op jit(solution)/shard_map/jit(cholesky)/cholesky | solution.py:67
  434.8 2.8 fusion.33
  437.7 11.2 %while.7 = (s32[]{:T(128)}, f32[512,512]{1,0:T(8,128)}, s32[4,2]{0,1:T(2,128)S(1)}, f32[4,128,128]{2,1,0:T(8,128)S(1)}, s32[]{:T(128)}) while((s32[]{:T(128)}, f32[512,512]{1,0:T(8,128)}, s32[4,2]{0,1:T(2,128)S(1)}, f32[4,128,128]{2,1,0:T(8,128)S(1)}, s32[]{:T(128)}) %tuple.75), condition=%wide.while_cond.2, body=%wide.while_body.2.sunk | while | flops 2 | bytes 131181 | solution.py:68
  438.3 2.2 bitcast_dynamic-update-slice_fusion.4
  441.1 2.2 bitcast_dynamic-update-slice_fusion.4
  444.0 2.2 bitcast_dynamic-update-slice_fusion.4
  446.8 2.1 bitcast_dynamic-update-slice_fusion.4
  449.6 40.1 %custom-call.30 = f32[4,128,128]{1,2,0:T(8,128)S(1)} custom-call(f32[4,128,128]{2,1,0:T(8,128)} %copy-done.9), custom_call_target="InvertDiagBlocksLowerTriangular" | custom-call | tf_op jit(solution)/shard_map/jit(_solve_triangular)/triangular_solve | solution.py:68
  495.8 14.3 %fusion.6 = f32[8,256,512]{2,1,0:T(8,128)S(1)} fusion(f32[8,256,512]{1,2,0:T(8,128)S(1)} %copy-done.3, f32[8]{0:T(128)S(1)} %get-tuple-element.116, f32[128,512]{1,0:T(8,128)S(1)} %fusion.81, f32[128,512]{1,0:T(8,128)S(1)} %fusion.82, f32[128,512]{1,0:T(8,128)S(1)} %fusion.84, f32[128,512]{1,0:T(8,128)S(1)} %fusion.59), kind=kOutput, calls=%fused_computation.12 | convolution fusion | flops 6444285952 | bytes 9437216 | tf_op jit(solution)/shard_map/dot_general | solution.py:72
  510.2 1.9 copy-done.1
  513.0 2.3 fusion.121
  515.3 5.3 copy.61
  520.6 2.1 copy.60
  522.7 2.0 copy.62
  524.8 5.1 multiply_add_fusion.1
  529.8 26.2 %all-reduce.8.cloned.1.call-done = f32[256,512]{1,0:T(8,128)} async-done(((f32[256,512]{1,0:T(8,128)}), f32[256,512]{1,0:T(8,128)}) %all-reduce.8.cloned.1.call-update) | async-done | bytes 524304 | tf_op jit(solution)/shard_map/psum | solution.py:12
  556.1 11.0 %broadcast_select_fusion = (f32[8,256,256]{1,2,0:T(8,128)}, f32[8,256,256]{1,2,0:T(8,128)}, f32[8,256,256]{1,2,0:T(8,128)}) fusion(pred[]{:T(512)S(6)} %eq.151, pred[]{:T(512)S(6)} %eq.132, f32[8,256,512]{2,1,0:T(8,128)} %copy-done.1, f32[256,512]{1,0:T(8,128)} %all-reduce.8.cloned.1.call-done, f32[8,256,256]{1,2,0:T(8,128)} %copy.57, ...), kind=kOutput, calls=%fused_computation.68 | convolution fusion | flops 3224895488 | bytes 19398668 | tf_op jit(solution)/shard_map/aep,bfp->abef/dot_general | solution.py:76
  567.2 111.4 %all-reduce.12.cloned.1.call-done = (f32[8,256,256]{1,2,0:T(8,128)}, f32[8,256,256]{1,2,0:T(8,128)}) async-done(((f32[8,256,256]{1,2,0:T(8,128)}, f32[8,256,256]{1,2,0:T(8,128)}), (f32[8,256,256]{1,2,0:T(8,128)}, f32[8,256,256]{1,2,0:T(8,128)})) %all-reduce.12.cloned.1.call-update) | async-done | bytes 4194320 | tf_op jit(solution)/shard_map/psum | solution.py:12
  678.6 1.9 constant_dynamic-update-slice_fusion.3
  681.0 1.9 copy-done.4
  684.0 31.6 %all-gather.7.cloned.1.call-done = f32[1,1024,512]{1,2,0:T(8,128)} async-done(((f32[1,256,512]{1,2,0:T(8,128)}), f32[1,1024,512]{1,2,0:T(8,128)}) %all-gather.7.cloned.1.call-update) | async-done | bytes 2097168 | tf_op jit(solution)/shard_map/all_gather | solution.py:64
  718.7 11.7 %cholesky.358 = f32[128,128]{1,0:T(8,128)S(1)} custom-call(f32[128,128]{1,0:T(8,128)S(1)} %cholesky.439), custom_call_target="Cholesky" | custom-call | tf_op jit(solution)/shard_map/jit(cholesky)/cholesky | solution.py:67
  730.6 9.8 %custom-call.31 = f32[1,128,128]{1,2,0:T(8,128)S(1)} custom-call(f32[1,128,128]{2,1,0:T(8,128)S(1)} %get-tuple-element.104), custom_call_target="InvertDiagBlocksLowerTriangular" | custom-call | tf_op jit(solution)/shard_map/jit(cholesky)/cholesky | solution.py:67
  741.0 11.7 %cholesky.377 = f32[128,128]{1,0:T(8,128)S(1)} custom-call(f32[128,128]{1,0:T(8,128)S(1)} %cholesky.443), custom_call_target="Cholesky" | custom-call | tf_op jit(solution)/shard_map/jit(cholesky)/cholesky | solution.py:67
  754.1 10.2 %custom-call.32 = f32[1,128,128]{1,2,0:T(8,128)S(1)} custom-call(f32[1,128,128]{2,1,0:T(8,128)S(1)} %get-tuple-element.101), custom_call_target="InvertDiagBlocksLowerTriangular" | custom-call | tf_op jit(solution)/shard_map/jit(cholesky)/cholesky | solution.py:67
  765.0 11.7 %cholesky.398 = f32[128,128]{1,0:T(8,128)S(1)} custom-call(f32[128,128]{1,0:T(8,128)S(1)} %cholesky.448), custom_call_target="Cholesky" | custom-call | tf_op jit(solution)/shard_map/jit(cholesky)/cholesky | solution.py:67
  777.4 9.8 %custom-call.33 = f32[1,128,128]{1,2,0:T(8,128)S(1)} custom-call(f32[1,128,128]{2,1,0:T(8,128)S(1)} %get-tuple-element.98), custom_call_target="InvertDiagBlocksLowerTriangular" | custom-call | tf_op jit(solution)/shard_map/jit(cholesky)/cholesky | solution.py:67
  787.8 11.7 %cholesky.415 = f32[128,128]{1,0:T(8,128)S(1)} custom-call(f32[128,128]{1,0:T(8,128)S(1)} %convolution_subtract_fusion.10), custom_call_target="Cholesky" | custom-call | tf_op jit(solution)/shard_map/jit(cholesky)/cholesky | solution.py:67
  804.2 11.8 %while.8 = (s32[]{:T(128)}, f32[512,512]{1,0:T(8,128)}, s32[4,2]{0,1:T(2,128)S(1)}, f32[4,128,128]{2,1,0:T(8,128)S(1)}, s32[]{:T(128)}) while((s32[]{:T(128)}, f32[512,512]{1,0:T(8,128)}, s32[4,2]{0,1:T(2,128)S(1)}, f32[4,128,128]{2,1,0:T(8,128)S(1)}, s32[]{:T(128)}) %tuple.95), condition=%wide.while_cond.2.clone, body=%wide.while_body.2.clone.sunk | while | flops 2 | bytes 131181 | solution.py:68
  804.9 2.3 bitcast_dynamic-update-slice_fusion.5
  807.9 2.3 bitcast_dynamic-update-slice_fusion.5
  810.8 2.3 bitcast_dynamic-update-slice_fusion.5
  813.8 2.2 bitcast_dynamic-update-slice_fusion.5
  816.0 39.3 %custom-call.34 = f32[4,128,128]{1,2,0:T(8,128)S(1)} custom-call(f32[4,128,128]{2,1,0:T(8,128)S(1)} %get-tuple-element.58), custom_call_target="InvertDiagBlocksLowerTriangular" | custom-call | tf_op jit(solution)/shard_map/jit(_solve_triangular)/triangular_solve | solution.py:68
  861.4 14.1 %fusion.4 = f32[8,256,512]{2,1,0:T(8,128)S(1)} fusion(f32[8,256,512]{1,2,0:T(8,128)S(1)} %copy-done.5, f32[8]{0:T(128)S(1)} %get-tuple-element.115, f32[128,512]{1,0:T(8,128)S(1)} %fusion.75, f32[128,512]{1,0:T(8,128)S(1)} %fusion.76, f32[128,512]{1,0:T(8,128)S(1)} %fusion.78, f32[128,512]{1,0:T(8,128)S(1)} %fusion.57), kind=kOutput, calls=%fused_computation.9 | convolution fusion | flops 6444285952 | bytes 9437216 | tf_op jit(solution)/shard_map/dot_general | solution.py:72
  875.5 1.9 copy-done
  878.4 5.4 copy.66
  884.2 4.8 multiply_add_fusion
  888.9 32.5 %all-reduce.10.cloned.1.call-done = f32[256,512]{1,0:T(8,128)} async-done(((f32[256,512]{1,0:T(8,128)}), f32[256,512]{1,0:T(8,128)}) %all-reduce.10.cloned.1.call-update) | async-done | bytes 524304 | tf_op jit(solution)/shard_map/psum | solution.py:12
  921.4 8.0 fusion.10
  929.4 3.6 copy.68
  (124 shorter events, 46.8 us)
Async XLA Ops:
  8.6 28.6 %all-to-all-start = ((f32[32,1,1]{2,1,0:T(1,128)}), f32[32,1,1]{2,1,0:T(1,128)S(1)}, u32[]{:S(2)}, u32[]{:S(2)}) async-start(f32[32,1,1]{2,1,0:T(1,128)} %bitcast.66), calls=%async_computation | async-start | bytes 32768 | tf_op jit(solution)/shard_map/all_to_all | solution.py:40
  37.2 131.5 %all-to-all-start.1 = ((f32[32,256,256]{2,1,0:T(8,128)}), f32[32,256,256]{2,1,0:T(8,128)}, u32[]{:S(2)}, u32[]{:S(2)}) async-start(f32[32,256,256]{2,1,0:T(8,128)} %copy.55), calls=%async_computation.1 | async-start | bytes 16777216 | tf_op jit(solution)/shard_map/all_to_all | solution.py:39
  44.6 253.4 %all-reduce.14.cloned.1.call-start = ((), (), s32[]{:S(2)}) async-start(), calls=%async_computation.7 | async-start | bytes 8388608 | tf_op jit(solution)/shard_map/psum | solution.py:12
  187.5 147.5 %all-gather.5.cloned.1.call-start = ((), (), s32[]{:S(2)}) async-start(), calls=%async_computation.4 | async-start | bytes 2621440 | tf_op jit(solution)/shard_map/all_gather | solution.py:64
  298.0 2.2 copy-start.7
  298.0 5.5 copy-start.10
  300.4 1.9 copy-start.2
  303.2 252.9 %all-reduce.8.cloned.1.call-start = ((), (), s32[]{:S(2)}) async-start(), calls=%async_computation.2 | async-start | bytes 1048576 | tf_op jit(solution)/shard_map/psum | solution.py:12
  341.6 1.0 copy-start.6
  448.9 0.7 copy-start.9
  489.8 6.1 copy-start.3
  510.2 1.9 copy-start.1
  513.0 165.6 %all-reduce.12.cloned.1.call-start = ((), (), s32[]{:S(2)}) async-start(), calls=%async_computation.6 | async-start | bytes 8388608 | tf_op jit(solution)/shard_map/psum | solution.py:12
  567.1 148.4 %all-gather.7.cloned.1.call-start = ((), (), s32[]{:S(2)}) async-start(), calls=%async_computation.5 | async-start | bytes 2621440 | tf_op jit(solution)/shard_map/all_gather | solution.py:64
  678.6 2.2 copy-start.8
  681.0 1.9 copy-start.4
  683.7 237.7 %all-reduce.10.cloned.1.call-start = ((), (), s32[]{:S(2)}) async-start(), calls=%async_computation.3 | async-start | bytes 1048576 | tf_op jit(solution)/shard_map/psum | solution.py:12
  855.3 6.1 copy-start.5
  875.5 1.9 copy-start
Sparse Core Ops, SparseCore 0:
  187.6 110.3 all-reduce.13
  303.3 31.6 all-gather.4
  513.1 42.9 all-reduce.7
  567.2 111.2 all-reduce.11
  683.9 31.6 all-gather.6
  878.4 42.9 all-reduce.9
where the time goes:
time: 950 us; the launch traced here: 940 us
  waiting for transfers between devices  462 us (49%)
  other arithmetic  263 us (28%)
  matrix products  94.8 us (10%)
  local copies, waits for them, and re-layouts  83.1 us (9%)
  between operations  20.2 us (2%)
  starting transfers between devices  16.2 us (2%)
    psum x4, waiting for transfers between devices, broadcast(): return lax.psum(block, axis)  281 us
    another operation x29, other arithmetic, local(): factor = jnp.linalg.cholesky(diagonal)  160 us
    all_to_all x1, waiting for transfers between devices, local(): lax.all_to_all(payload, 'col', split_axis=0, concat_axis=0, tiled=True)  119 us
    another operation x5, other arithmetic, local(): inverse = jax.scipy.linalg.solve_triangular(factor, ident, lower=True)  83.5 us
    all_gather x2, waiting for transfers between devices, local(): near = lax.all_gather(panel[lead], 'row', axis=0, tiled=True)  62.7 us
    dot_general x2, matrix products, local(): jnp.dot(masked.reshape(rows_t * tile, PANEL), inverse.T, precision=highest)  28.4 us
    another operation x27, local copies, waits for them, and re-layouts, local(): inverse = jax.scipy.linalg.solve_triangular(factor, ident, lower=True)  22.9 us
    dot_general x2, matrix products, local(): jnp.einsum('aep,bfp->abef', lower, across, precision=highest)  19 us
  transfers between devices with their start and end apart: 8, of which 7 were waited for; matrix products, arithmetic and copies ran while one was open for 6% of the time, Pallas kernels for 0%

commit v1 on v0

v1 whole, which is shorter than its diff:
```python
import jax
import jax.numpy as jnp
from jax import lax
from jax.experimental import pallas as pl
from jax.experimental.pallas import tpu as pltpu
from jax.sharding import PartitionSpec as P

HI = lax.Precision.HIGHEST
NB = 128
SB = 32
TILE = 256
MIB = 1024 * 1024

def dot_nt(a, b):
    return lax.dot_general(a, b, (((1,), (1,)), ((), ())), precision=HI, preferred_element_type=jnp.float32)

def dot_tn(a, b):
    return lax.dot_general(a, b, (((0,), (0,)), ((), ())), precision=HI, preferred_element_type=jnp.float32)

def invert_factor(block):
    sub = lax.broadcasted_iota(jnp.int32, (NB, NB), 0)
    lane = lax.broadcasted_iota(jnp.int32, (NB, NB), 1)
    eye = (sub == lane).astype(jnp.float32)
    rest = jnp.concatenate([block, eye], axis=1)
    done = []
    for sb in range(NB // SB):
        w = rest[:SB]
        rows = []
        for t in range(SB // 8):
            base = sb * SB + t * 8
            h = w.shape[0]
            ids = lax.broadcasted_iota(jnp.int32, (h, NB), 0)
            cols = [jnp.broadcast_to(w[:, base + i:base + i + 1], (h, NB)) for i in range(8)]
            final = []
            for j in range(8):
                cj = cols[j]
                piv = jnp.broadcast_to(cj[j:j + 1], (8, NB))
                rs = lax.rsqrt(piv)
                rs_h = jnp.concatenate([rs] * (h // 8), axis=0)
                inv = rs * rs
                inv_h = jnp.concatenate([inv] * (h // 8), axis=0)
                for i in range(j + 1, 8):
                    ci = jnp.broadcast_to(cj[i:i + 1], (h, NB))
                    cols[i] = cols[i] - cj * (ci * inv_h)
                lj = jnp.where(ids > j, cj * rs_h, 0.0)
                r = w[j:j + 1] * jnp.concatenate([rs[:1], rs[:1]], axis=1)
                final.append(r)
                lw = jnp.concatenate([lj, lj], axis=1)
                w = w - lw * jnp.broadcast_to(r, (h, 2 * NB))
            rows.append(jnp.concatenate(final, axis=0))
            w = w[8:]
        r = jnp.concatenate(rows, axis=0)
        done.append(r[:, NB:])
        if sb + 1 < NB // SB:
            lo = (sb + 1) * SB
            rest = rest[SB:] - dot_tn(r[:, lo:NB], r)
    return jnp.concatenate(done, axis=0)

def chol_body(where_ref, diag_ref, own_ref, out_ref, s):
    n = diag_ref.shape[0]
    m = own_ref.shape[0]
    nb = n // NB
    half = nb // 2
    for a in range(nb):
        for b in range(a + 1):
            x = diag_ref[a * NB:(a + 1) * NB, b * NB:(b + 1) * NB]
            if a // half == b // half:
                y = diag_ref[b * NB:(b + 1) * NB, a * NB:(a + 1) * NB]
                x = (x + y.T) * 0.5
            s[a * NB:(a + 1) * NB, b * NB:(b + 1) * NB] = x
        if a + 1 < nb:
            s[a * NB:(a + 1) * NB, (a + 1) * NB:] = jnp.zeros((NB, n - (a + 1) * NB), jnp.float32)
    row0 = where_ref[0]
    s[n:n + 8, :] = s[pl.ds(pl.multiple_of(row0, 8), 8), :]
    for t in range(1, m // 8):
        s[n + 8 * t:n + 8 * t + 8, :] = jnp.where(where_ref[t] > 0, own_ref[8 * t:8 * t + 8, :], 0.0)
    for k in range(nb):
        lo = k * NB
        hi = lo + NB
        inv = invert_factor(s[lo:hi, lo:hi])
        x = dot_nt(s[hi:, lo:hi], inv)
        s[hi:, lo:hi] = x
        at = hi
        while at < n:
            width = NB if at == hi else min(2 * NB, n - at)
            s[at:, at:at + width] = s[at:, at:at + width] - dot_nt(x[at - hi:], x[at - hi:at - hi + width])
            at += width
    res = s[n:, :]
    ids = lax.broadcasted_iota(jnp.int32, (m, n), 0)
    lane = lax.broadcasted_iota(jnp.int32, (m, n), 1)
    out_ref[...] = jnp.where((ids >= 8) | (lane <= ids + row0), res, 0.0)

def chol_call(where, diag, own):
    n, m = diag.shape[0], own.shape[0]
    return pl.pallas_call(
        chol_body,
        out_shape=jax.ShapeDtypeStruct((m, n), jnp.float32),
        in_specs=[pl.BlockSpec(memory_space=pltpu.SMEM), pl.BlockSpec(memory_space=pltpu.VMEM), pl.BlockSpec(memory_space=pltpu.VMEM)],
        out_specs=pl.BlockSpec(memory_space=pltpu.VMEM),
        scratch_shapes=[pltpu.VMEM((n + m, n), jnp.float32)],
        compiler_params=pltpu.CompilerParams(vmem_limit_bytes=32 * 1024 * 1024),
        cost_estimate=pl.CostEstimate(flops=60_000_000_000, bytes_accessed=5_000_000, transcendentals=0),
    )(where, diag, own)


def pack_body(slot_ref, tile_ref, out_ref):
    out_ref[...] = tile_ref[...]


def pack_call(slots, tiles):
    n = slots.shape[0]
    t = tiles.shape[1]
    return pl.pallas_call(
        pack_body,
        out_shape=jax.ShapeDtypeStruct((n, t, t), tiles.dtype),
        grid_spec=pltpu.PrefetchScalarGridSpec(
            num_scalar_prefetch=1,
            grid=(n,),
            in_specs=[pl.BlockSpec((1, t, t), lambda q, slot: (slot[q], 0, 0))],
            out_specs=pl.BlockSpec((1, t, t), lambda q, slot: (q, 0, 0)),
        ),
        cost_estimate=pl.CostEstimate(flops=0, bytes_accessed=n * t * t * 8, transcendentals=0),
    )(slots, tiles)


def panel_body(got_ref, front_ref, out_ref):
    sources, slab, _ = got_ref.shape
    lead = front_ref.shape[1]
    for q in range(4):
        at = slice(q * TILE, (q + 1) * TILE)
        acc = [front_ref[q, t] for t in range(lead)]
        for s in range(sources):
            label = got_ref[s, q:q + 1, 5 * TILE:5 * TILE + 128]
            label = jnp.broadcast_to(jnp.concatenate([label, label], axis=1), (slab, TILE))
            part = got_ref[s, :, at]
            for t in range(lead):
                acc[t] = acc[t] + jnp.where(label == float(t), part, 0.0)
        for t in range(lead):
            out_ref[t * slab:(t + 1) * slab, at] = acc[t]


def panel_call(got, front_part):
    lead, slab = front_part.shape[1], front_part.shape[2]
    return pl.pallas_call(
        panel_body,
        out_shape=jax.ShapeDtypeStruct((lead * slab, 4 * TILE), jnp.float32),
        cost_estimate=pl.CostEstimate(flops=0, bytes_accessed=got.size * 4, transcendentals=0),
    )(got, front_part)


def add_body(label_ref, front_ref, got_ref, out_ref):
    out_ref[...] = front_ref[...]

    def step(s, carry):
        p = label_ref[s]

        @pl.when(p >= 0)
        def _():
            out_ref[p] = out_ref[p] + got_ref[s]

        return carry

    lax.fori_loop(0, got_ref.shape[0], step, 0)


def add_call(labels, front, got):
    lead = front.shape[0]
    n = got.shape[0]
    rows = 32
    return pl.pallas_call(
        add_body,
        out_shape=jax.ShapeDtypeStruct(front.shape, jnp.float32),
        grid_spec=pltpu.PrefetchScalarGridSpec(
            num_scalar_prefetch=1,
            grid=(TILE // rows,),
            in_specs=[
                pl.BlockSpec((lead, rows, TILE), lambda i, _: (0, i, 0)),
                pl.BlockSpec((n, rows, TILE), lambda i, _: (0, i, 0)),
            ],
            out_specs=pl.BlockSpec((lead, rows, TILE), lambda i, _: (0, i, 0)),
        ),
        cost_estimate=pl.CostEstimate(flops=0, bytes_accessed=(n + 2 * lead) * TILE * TILE * 4, transcendentals=0),
    )(labels, front, got)


def split(x):
    high = x.astype(jnp.bfloat16)
    low = (x - high.astype(jnp.float32)).astype(jnp.bfloat16)
    return high, low


def nt(a, b):
    return lax.dot_general(a, b, (((1,), (1,)), ((), ())), preferred_element_type=jnp.float32)


def final_body(col_ref, acc_ref, l_ref, across_ref, out_ref):
    c = col_ref[0]
    t = pl.program_id(0)
    n = across_ref.shape[1]

    @pl.when(c < 4)
    def _():
        at = pl.multiple_of(jnp.minimum(c, 3) * TILE, TILE)
        out_ref[0] = l_ref[:, 0, :, pl.ds(at, TILE)].reshape(TILE, TILE)

    @pl.when((c >= 4) & (t == 0))
    def _():
        out_ref[...] = jnp.zeros_like(out_ref)

    @pl.when((c >= 4) & (t > 0))
    def _():
        ah, al = split(l_ref[...].reshape(TILE, n))
        bh, bl = split(across_ref[...])
        out_ref[0] = acc_ref[0] - (nt(ah, bh) + (nt(ah, bl) + nt(al, bh)))


def final_call(col, acc, gathered, across):
    lead = acc.shape[0]
    j, _, slab, n = gathered.shape
    return pl.pallas_call(
        final_body,
        out_shape=jax.ShapeDtypeStruct(acc.shape, jnp.float32),
        grid_spec=pltpu.PrefetchScalarGridSpec(
            num_scalar_prefetch=1,
            grid=(lead,),
            in_specs=[
                pl.BlockSpec((1, TILE, TILE), lambda i, _: (i, 0, 0)),
                pl.BlockSpec((j, 1, slab, n), lambda i, _: (0, i, 0, 0)),
                pl.BlockSpec((TILE, n), lambda i, _: (0, 0)),
            ],
            out_specs=pl.BlockSpec((1, TILE, TILE), lambda i, _: (i, 0, 0)),
        ),
        compiler_params=pltpu.CompilerParams(vmem_limit_bytes=32 * MIB),
        cost_estimate=pl.CostEstimate(flops=6 * lead * TILE * TILE * n, bytes_accessed=gathered.size * 4, transcendentals=0),
    )(col, acc, gathered, across)


def local(front, child_tiles, child_owner, child_place, child_count, tile_mask):
    n_row = lax.axis_size("row")
    n_col = lax.axis_size("col")
    row_id = lax.axis_index("row")
    col_id = lax.axis_index("col")
    lead = front.shape[0]
    slab = TILE // n_col
    slots = child_tiles.shape[2]
    blocks = front.reshape(lead, TILE, TILE)
    tiles = child_tiles.reshape(slots, TILE, TILE)
    owner = child_owner.reshape(slots)
    place = child_place.reshape(slots)
    count = child_count.reshape(())
    ids = jnp.arange(slots, dtype=jnp.int32)
    hit = owner[None, :] == jnp.arange(n_col, dtype=jnp.int32)[:, None]
    slot_of = jnp.sum(jnp.where(hit, ids[None, :], 0), axis=1)
    label = jnp.sum(jnp.where(hit & (ids < count)[None, :], place[None, :] + 1, 0), axis=1) - 1
    label_f = label.astype(jnp.float32)

    panel_tiles = pack_call(slot_of[:4], tiles)
    slabs = panel_tiles.reshape(4, n_col, slab, TILE).transpose(1, 2, 0, 3).reshape(n_col, slab, 4 * TILE)
    mirrored = blocks[0].T.reshape(n_col, slab, TILE)
    marks = jnp.concatenate(
        [jnp.broadcast_to(label_f[None, :4], (n_col, 4)), label_f[:, None], jnp.zeros((n_col, slab - 5), jnp.float32)], axis=1
    )
    marks = jnp.broadcast_to(marks[:, :, None], (n_col, slab, 128))
    message = jnp.concatenate([slabs, mirrored, marks], axis=2)
    got = lax.all_to_all(message, "col", split_axis=0, concat_axis=0, tiled=True)
    cross = got[:, :, 4 * TILE:5 * TILE].reshape(lead, n_row, slab, TILE).transpose(1, 0, 2, 3)
    cross = lax.all_to_all(cross, "row", split_axis=0, concat_axis=0, tiled=True)
    own = panel_call(got, cross)

    payload = pack_call(slot_of, tiles)
    payload, got = lax.optimization_barrier((payload, got))
    arrived = lax.all_to_all(payload, "col", split_axis=0, concat_axis=0, tiled=True)

    diag = lax.all_gather(own[:slab], ("row", "col"), axis=0, tiled=True)
    row_tiles = jnp.arange(lead, dtype=jnp.int32) * n_row + row_id
    keep = jnp.sum(jnp.where(row_tiles[:, None] == jnp.arange(tile_mask.shape[0])[None, :], tile_mask[None, :], 0), axis=1)
    where = jnp.concatenate([(row_id * TILE + col_id * slab)[None], keep[1:]]).astype(jnp.int32)
    mine = chol_call(where, diag, own)
    gathered = lax.all_gather(mine, "col", axis=0, tiled=False).reshape(n_col, lead, slab, 4 * TILE)
    chosen = lax.dynamic_slice_in_dim(gathered, col_id // n_row, 1, axis=1).reshape(TILE, 4 * TILE)
    across = lax.psum(jnp.where(row_id == col_id % n_row, chosen, 0.0), "row")

    got_labels = got[:, 4, 5 * TILE].astype(jnp.int32)
    acc = add_call(got_labels, blocks, arrived)
    result = final_call(col_id.reshape(1), acc, gathered, across)
    return result.reshape(front.shape)


def solution(mesh):
    return jax.shard_map(
        local,
        mesh=mesh,
        in_specs=(
            P(None, "row", None, None, "col", None),
            P("row", "col", None, None, None),
            P("row", "col", None),
            P("row", "col", None),
            P("row", "col"),
            P(),
        ),
        out_specs=P(None, "row", None, None, "col", None),
        check_vma=False,
    )
```

time: 950 us -> 378 us (0.40)
  other arithmetic: 263 us -> 6.93 us
  waiting for transfers between devices: 462 us -> 206 us
  matrix products: 94.8 us -> 0 us
  Pallas kernels: 0 us -> 84.8 us
  local copies, waits for them, and re-layouts: 83.1 us -> 18.7 us
  blocking collectives: 0 us -> 37.8 us
    another operation x36 -> x0, other arithmetic: 246 us -> none  [the longest x29 160 us: local(): factor = jnp.linalg.cholesky(diagonal)]
    psum x4 -> x1, waiting for transfers between devices: 281 us -> 36.2 us  [local(): across = lax.psum(jnp.where(row_id == col_id % n_row, chosen, 0.0), 'row')]
    all_to_all x1, waiting for transfers between devices: 119 us -> 1.68 us  [local(): lax.all_to_all(payload, 'col', split_axis=0, concat_axis=0, tiled=True)]
    all_gather x2, waiting for transfers between devices: 62.7 us -> 168 us  [the longest x1 106 us: local(): lax.all_gather(mine, 'col', axis=0, tiled=False)]
    pallas_call x0 -> x6, Pallas kernels: none -> 84.8 us  [the longest x1 42.8 us: chol_call(): pl.pallas_call(chol_body, out_shape=jax.ShapeDtypeStruct((m, n), jnp.floa...]
    dot_general x7 -> x0, matrix products: 73.1 us -> none  [the longest x2 28.4 us: local(): jnp.dot(masked.reshape(rows_t * tile, PANEL), inverse.T, precision=highest)]
    all_to_all x0 -> x2, blocking collectives: none -> 37.8 us  [the longest x1 26.2 us: local(): lax.all_to_all(message, 'col', split_axis=0, concat_axis=0, tiled=True)]
    another operation x36 -> x0, local copies, waits for them, and re-layouts: 27.7 us -> none  [the longest x27 22.9 us: local(): inverse = jax.scipy.linalg.solve_triangular(factor, ident, lower=True)]
  transfers between devices with their start and end apart: 8 -> 4, of which waited for: 7 -> 4; matrix products, arithmetic and copies ran while one was open for 6% -> 2% of each run, Pallas kernels for 0% -> 8%
where the time goes in v1:
time: 378 us; the launch traced here: 376 us
  waiting for transfers between devices  206 us (54%)
  Pallas kernels  84.8 us (22%)
  blocking collectives  37.8 us (10%)
  local copies, waits for them, and re-layouts  18.7 us (5%)
  between operations  13.9 us (4%)
  starting transfers between devices  7.76 us (2%)
  other arithmetic  6.93 us (2%)
    all_gather x1, waiting for transfers between devices, local(): lax.all_gather(mine, 'col', axis=0, tiled=False)  106 us
    all_gather x1, waiting for transfers between devices, local(): diag = lax.all_gather(own[:slab], ('row', 'col'), axis=0, tiled=True)  62.7 us
    pallas_call x1, Pallas kernels, chol_call(): pl.pallas_call(chol_body, out_shape=jax.ShapeDtypeStruct((m, n), jnp.floa...  42.8 us
    psum x1, waiting for transfers between devices, local(): across = lax.psum(jnp.where(row_id == col_id % n_row, chosen, 0.0), 'row')  36.2 us
    all_to_all x1, blocking collectives, local(): lax.all_to_all(message, 'col', split_axis=0, concat_axis=0, tiled=True)  26.2 us
    pallas_call x2, Pallas kernels, pack_call(): pl.pallas_call(pack_body, out_shape=jax.ShapeDtypeStruct((n, t, t), tiles...  24 us
    all_to_all x1, blocking collectives, local(): lax.all_to_all(cross, 'row', split_axis=0, concat_axis=0, tiled=True)  11.6 us
    unnamed x17, local copies, waits for them, and re-layouts  10.9 us
  transfers between devices with their start and end apart: 4, of which 4 were waited for; matrix products, arithmetic and copies ran while one was open for 2% of the time, Pallas kernels for 8%

profile of v1, /device:TPU:48, one launch (start us, length us, event | category | flops | bytes accessed | tf_op | source)
XLA Modules:
  0.0 376.1 jit_solution(6818298814920461389)
XLA Ops:
  6.5 0.0 all-gather.4.cloned.1.call-start
  6.5 0.7 add_bitcast_fusion
  7.9 1.3 select_reduce_fusion
  9.2 0.1 pad.7.clone
  9.3 0.1 maximum_maximum_fusion
  9.4 0.1 copy.23
  9.5 1.1 slice.23
  10.6 0.1 copy.28
  10.7 4.0 %shard_map.65 = f32[4,256,256]{2,1,0:T(8,128)} custom-call(s32[4]{0:T(128)} %bitcast.44, f32[32,256,256]{2,1,0:T(8,128)} %bitcast.36), custom_call_target="tpu_custom_call" | custom-call | bytes 2097152 | tf_op jit(solution)/shard_map/pallas_call | solution.py:113
  14.8 1.3 copy.21
  16.1 0.1 broadcast_in_dim.64
  16.2 0.1 pad_maximum_fusion
  16.3 26.2 %all_to_all.15.got_ref = f32[32,8,1408]{2,1,0:T(8,128)S(1)} all-to-all(f32[32,8,1408]{2,1,0:T(8,128)S(1)} %pad_maximum_fusion), channel_id=1, replica_groups=mesh['row'=4,'col'=32] {'col'}, dimensions={0} | all-to-all | bytes 2883584 | tf_op jit(solution)/shard_map/all_to_all | solution.py:265
  42.5 0.0 copy-start.5
  42.5 0.0 copy-start.7
  42.5 11.6 %all_to_all.16.front_ref = f32[4,8,8,256]{3,2,1,0:T(8,128)} all-to-all(f32[4,8,8,256]{3,2,1,0:T(8,128)S(1)} %bitcast.41), channel_id=1, replica_groups=mesh['row'=4,'col'=32] {'row'}, dimensions={0} | all-to-all | bytes 524288 | tf_op jit(solution)/shard_map/all_to_all | solution.py:267
  54.2 0.0 copy-done.5
  54.2 2.8 shard_map.67.own_ref
  57.0 1.4 slice.30
  58.4 0.0 all-gather.4.cloned.1.call-update
  58.4 0.2 all-gather.6.cloned.1.call-start
  58.7 0.0 copy-done.7
  58.7 0.2 select_reduce_fusion.2
  58.9 0.1 slice.26
  58.9 0.1 pad_add_fusion.where_ref
  59.0 62.7 %all-gather.4.cloned.1.call-done.diag_ref = f32[1024,1024]{1,0:T(8,128)} async-done(((f32[8,1024]{1,0:T(8,128)}), f32[1024,1024]{1,0:T(8,128)}) %all-gather.4.cloned.1.call-update) | async-done | bytes 4194320 | tf_op jit(solution)/shard_map/all_gather | solution.py:274
  121.7 0.0 copy-start.3
  121.7 0.9 copy-done.3
  122.6 0.0 copy-start.4
  122.6 2.2 copy-done.4
  124.8 42.8 %shard_map.68 = f32[64,1024]{1,0:T(8,128)} custom-call(s32[8]{0:T(128)S(1)} %pad_add_fusion.where_ref, f32[1024,1024]{1,0:T(8,128)S(1)} %copy-done.4, f32[64,1024]{1,0:T(8,128)S(1)} %copy-done.3), custom_call_target="tpu_custom_call" | custom-call | flops 60000002048 | bytes 5000000 | tf_op jit(solution)/shard_map/pallas_call | solution.py:95
  167.6 0.0 all-gather.6.cloned.1.call-update
  167.7 19.9 %shard_map.64 = f32[32,256,256]{2,1,0:T(8,128)} custom-call(s32[32]{0:T(128)} %get-tuple-element.10.slot_ref, f32[32,256,256]{2,1,0:T(8,128)} %bitcast.37), custom_call_target="tpu_custom_call" | custom-call | bytes 16777216 | tf_op jit(solution)/shard_map/pallas_call | solution.py:113
  187.6 7.2 %all-to-all-start.1 = ((f32[32,256,256]{2,1,0:T(8,128)}), f32[32,256,256]{2,1,0:T(8,128)}, u32[]{:S(2)}, u32[]{:S(2)}) async-start(f32[32,256,256]{2,1,0:T(8,128)} %shard_map.64), calls=%async_computation.1 | async-start | bytes 16777216 | tf_op jit(solution)/shard_map/all_to_all | solution.py:272
  194.8 0.0 copy-start.6
  194.8 0.3 all-reduce.2.cloned.1.call-start
  195.2 105.6 %all-gather.6.cloned.1.call-done = f32[2048,1024]{1,0:T(8,128)} async-done(((f32[64,1024]{1,0:T(8,128)}), f32[2048,1024]{1,0:T(8,128)}) %all-gather.6.cloned.1.call-update) | async-done | bytes 8388624 | tf_op jit(solution)/shard_map/all_gather | solution.py:279
  300.8 2.3 select_bitcast_fusion
  303.1 0.0 all-reduce.2.cloned.1.call-update
  303.1 0.0 copy-done.6
  303.1 1.5 copy.31
  304.7 2.1 convert_reduce_fusion.label_ref
  306.8 1.7 all-to-all-done.1.got_ref
  308.5 10.0 %shard_map.66.acc_ref = f32[8,256,256]{2,1,0:T(8,128)} custom-call(s32[32]{0:T(128)} %convert_reduce_fusion.label_ref, f32[8,256,256]{2,1,0:T(8,128)} %bitcast.38, f32[32,256,256]{2,1,0:T(8,128)} %all-to-all-done.1.got_ref), custom_call_target="tpu_custom_call" | custom-call | bytes 12582912 | tf_op jit(solution)/shard_map/pallas_call | solution.py:170
  318.5 36.2 %all-reduce.2.cloned.1.call-done.across_ref = f32[256,1024]{1,0:T(8,128)} async-done(((f32[256,1024]{1,0:T(8,128)}), f32[256,1024]{1,0:T(8,128)}) %all-reduce.2.cloned.1.call-update) | async-done | bytes 1048592 | tf_op jit(solution)/shard_map/psum | solution.py:281
  354.6 0.0 copy-start
  354.6 3.4 copy-done
  358.0 0.0 copy-start.1
  358.0 1.6 copy-done.1
  359.6 0.0 copy-start.2
  359.6 1.2 copy-done.2
  360.8 5.2 %shard_map.69 = f32[8,256,256]{2,1,0:T(8,128)S(1)} custom-call(s32[1]{0:T(128)} %bitcast.col_ref, f32[8,256,256]{2,1,0:T(8,128)S(1)} %copy-done.1, f32[32,8,8,1024]{3,2,1,0:T(8,128)S(1)} %bitcast.34, f32[256,1024]{1,0:T(8,128)S(1)} %copy-done.2), custom_call_target="tpu_custom_call" | custom-call | flops 3221225472 | bytes 8388608 | tf_op jit(solution)/shard_map/pallas_call | solution.py:220
  366.0 3.5 copy.25
  (7 shorter events, 0.1 us)
Async XLA Ops:
  6.5 115.2 %all-gather.4.cloned.1.call-start = ((), (), s32[]{:S(2)}) async-start(), calls=%async_computation.3 | async-start | bytes 4227072 | tf_op jit(solution)/shard_map/all_gather | solution.py:274
  42.5 11.7 %copy-start.5 = (f32[32,8,1408]{2,1,0:T(8,128)}, f32[32,8,1408]{2,1,0:T(8,128)S(1)}, u32[]{:S(2)}) copy-start(f32[32,8,1408]{2,1,0:T(8,128)S(1)} %all_to_all.15.got_ref) | copy-start | bytes 4325380
  42.5 16.2 %copy-start.7 = (s32[32]{0:T(128)S(1)}, s32[32]{0:T(128)}, u32[]{:S(2)}) copy-start(s32[32]{0:T(128)} %param.11) | copy-start | bytes 388
  58.4 242.3 %all-gather.6.cloned.1.call-start = ((), (), s32[]{:S(2)}) async-start(), calls=%async_computation.5 | async-start | bytes 8650752 | tf_op jit(solution)/shard_map/all_gather | solution.py:279
  121.7 0.9 copy-start.3
  122.6 2.2 copy-start.4
  187.6 120.9 %all-to-all-start.1 = ((f32[32,256,256]{2,1,0:T(8,128)}), f32[32,256,256]{2,1,0:T(8,128)}, u32[]{:S(2)}, u32[]{:S(2)}) async-start(f32[32,256,256]{2,1,0:T(8,128)} %shard_map.64), calls=%async_computation.1 | async-start | bytes 16777216 | tf_op jit(solution)/shard_map/all_to_all | solution.py:272
  194.8 108.3 %copy-start.6 = (f32[8,1,256,1,1,256]{5,4,3,2,1,0:T(1,128)S(1)}, f32[8,1,256,1,1,256]{5,4,3,2,1,0:T(1,128)}, u32[]{:S(2)}) copy-start(f32[8,1,256,1,1,256]{5,4,3,2,1,0:T(1,128)} %param.6) | copy-start | bytes 6291460
  194.8 159.8 %all-reduce.2.cloned.1.call-start = ((), (), s32[]{:S(2)}) async-start(), calls=%async_computation.4 | async-start | bytes 2097152 | tf_op jit(solution)/shard_map/psum | solution.py:281
  354.6 3.4 copy-start
  358.0 1.6 copy-start.1
  359.6 1.2 copy-start.2
Sparse Core Ops, SparseCore 0:
  58.5 63.0 all-gather.3
  167.8 132.9 all-gather.5
  303.2 51.3 all-reduce.1

commit v2 on v1

--- a/solution.py
+++ b/solution.py
@@ -10,6 +10,7 @@
 SB = 32
 TILE = 256
 MIB = 1024 * 1024
+LATE = True
 
 def dot_nt(a, b):
     return lax.dot_general(a, b, (((1,), (1,)), ((), ())), precision=HI, preferred_element_type=jnp.float32)
@@ -56,8 +57,13 @@
             rest = rest[SB:] - dot_tn(r[:, lo:NB], r)
     return jnp.concatenate(done, axis=0)
 
-def chol_body(where_ref, diag_ref, own_ref, out_ref, s):
+def chol_body(where_ref, part_ref, own_ref, out_ref, s, diag_ref):
     n = diag_ref.shape[0]
+    for q in range(4):
+        rows = slice(q * TILE, (q + 1) * TILE)
+        diag_ref[rows, :2 * TILE] = part_ref[:, :, :, q].reshape(TILE, 2 * TILE)
+        if q >= 2:
+            diag_ref[rows, 2 * TILE:] = part_ref[:, :, :, 2 + q].reshape(TILE, 2 * TILE)
     m = own_ref.shape[0]
     nb = n // NB
     half = nb // 2
@@ -90,17 +96,306 @@
     lane = lax.broadcasted_iota(jnp.int32, (m, n), 1)
     out_ref[...] = jnp.where((ids >= 8) | (lane <= ids + row0), res, 0.0)
 
-def chol_call(where, diag, own):
-    n, m = diag.shape[0], own.shape[0]
+def chol_call(where, parts, own):
+    m, n = own.shape
+    vmem = pl.BlockSpec(memory_space=pltpu.VMEM)
     return pl.pallas_call(
         chol_body,
         out_shape=jax.ShapeDtypeStruct((m, n), jnp.float32),
-        in_specs=[pl.BlockSpec(memory_space=pltpu.SMEM), pl.BlockSpec(memory_space=pltpu.VMEM), pl.BlockSpec(memory_space=pltpu.VMEM)],
-        out_specs=pl.BlockSpec(memory_space=pltpu.VMEM),
-        scratch_shapes=[pltpu.VMEM((n + m, n), jnp.float32)],
-        compiler_params=pltpu.CompilerParams(vmem_limit_bytes=32 * 1024 * 1024),
-        cost_estimate=pl.CostEstimate(flops=60_000_000_000, bytes_accessed=5_000_000, transcendentals=0),
-    )(where, diag, own)
+        in_specs=[pl.BlockSpec(memory_space=pltpu.SMEM), vmem, vmem],
+        out_specs=vmem,
+        scratch_shapes=[pltpu.VMEM((n + m, n), jnp.float32), pltpu.VMEM((n, n), jnp.float32)],
+        compiler_params=pltpu.CompilerParams(vmem_limit_bytes=56 * MIB),
+        cost_estimate=pl.CostEstimate(flops=0, bytes_accessed=1000, transcendentals=0),
+    )(where, parts, own)
+
+
+MESH = pl.DeviceIdType.MESH
+
+
+def here():
+    r = lax.axis_index("row")
+    c = lax.axis_index("col")
+    return r, c, lax.div(c, 8), lax.rem(lax.div(c, 2), 4), lax.rem(c, 2)
+
+
+def at_col(y, z, k):
+    return (y * 4 + z) * 2 + k
+
+
+def turn(i, d):
+    return lax.rem(i + d, 4)
+
+
+def greet(devices):
+    barrier = pltpu.get_barrier_semaphore()
+    for device in devices:
+        pl.semaphore_signal(barrier, inc=1, device_id=device, device_id_type=MESH)
+    pl.semaphore_wait(barrier, len(devices))
+
+
+def plane_peers(r, y, z, k):
+    out = [(r, at_col(y, z, 1 - k))]
+    for d in range(1, 4):
+        out.append((r, at_col(y, turn(z, d), k)))
+        out.append((r, at_col(turn(y, d), z, k)))
+    return out
+
+
+def row_peers(r, c):
+    return [(turn(r, d), c) for d in range(1, 4)]
+
+
+def plane_gather(piece, send, recv, core_send, core_recv, r, y, z, k):
+    def place(h, a, b):
+        return (b, a) if h == 0 else (a, b)
+
+    def axes(h):
+        return (z, y) if h == 0 else (y, z)
+
+    def push(h, da, db, to, send_sem, recv_sem):
+        a, b = axes(h)
+        ref = piece(h, *place(h, turn(a, 4 - da), turn(b, 4 - db)), k)
+        copy = pltpu.make_async_remote_copy(
+            src_ref=ref, dst_ref=ref, send_sem=send_sem, recv_sem=recv_sem, device_id=to, device_id_type=MESH
+        )
+        copy.start()
+        return copy
+
+    def along_first(h, d):
+        a, b = axes(h)
+        yy, zz = place(h, turn(a, d), b)
+        return push(h, 0, 0, (r, at_col(yy, zz, k)), send.at[h, d, 0], recv.at[h, d, 0])
+
+    def along_second(h, da, d):
+        a, b = axes(h)
+        yy, zz = place(h, a, turn(b, d))
+        return push(h, da, 0, (r, at_col(yy, zz, k)), send.at[h, da, d], recv.at[h, da, d])
+
+    def across(h, da, db):
+        return push(h, da, db, (r, at_col(y, z, 1 - k)), core_send.at[h, da, db], core_recv.at[h, da, db])
+
+    first, second, core = {}, {}, {}
+    for d in range(1, 4):
+        for h in range(2):
+            first[h, d] = along_first(h, d)
+    for d in range(1, 4):
+        for h in range(2):
+            second[h, 0, d] = along_second(h, 0, d)
+    for h in range(2):
+        core[h, 0, 0] = across(h, 0, 0)
+    for da in range(1, 4):
+        for h in range(2):
+            first[h, da].wait_recv()
+            for d in range(1, 4):
+                second[h, da, d] = along_second(h, da, d)
+            core[h, da, 0] = across(h, da, 0)
+    for da in range(4):
+        for db in range(1, 4):
+            for h in range(2):
+                second[h, da, db].wait_recv()
+                core[h, da, db] = across(h, da, db)
+
+    def finish():
+        for copy in core.values():
+            copy.wait_recv()
+        for group in (first, second, core):
+            for copy in group.values():
+                copy.wait_send()
+
+    return finish
+
+
+def gather_sems():
+    return [pltpu.SemaphoreType.DMA((2, 4, 4)) for _ in range(4)]
+
+
+def rows_body(mine_ref, g_ref, across_ref, send, recv, core_send, core_recv, local_sem, x_send, x_recv):
+    r, c, y, z, k = here()
+    greet(plane_peers(r, y, z, k) + row_peers(r, c))
+    keep = pltpu.make_async_copy(mine_ref, g_ref.at[y, z, k], local_sem.at[0])
+    keep.start()
+    keep.wait()
+    half = mine_ref.shape[0] // 2
+
+    def piece(h, yy, zz, kk):
+        return g_ref.at[yy, zz, kk, pl.ds(h * half, half)]
+
+    finish = plane_gather(piece, send, recv, core_send, core_recv, r, y, z, k)
+    t = lax.div(c, 4)
+    source = lax.rem(c, 4)
+
+    def slab(kk):
+        return g_ref.at[:, :, kk, t]
+
+    def cross(i, kk, d):
+        return pltpu.make_async_remote_copy(
+            src_ref=slab(kk),
+            dst_ref=across_ref.at[:, :, kk],
+            send_sem=x_send.at[i, d],
+            recv_sem=x_recv.at[i],
+            device_id=(turn(r, d), c),
+            device_id_type=MESH,
+        )
+
+    @pl.when(r == source)
+    def _():
+        for d in range(1, 4):
+            cross(0, k, d).start()
+
+    finish()
+
+    @pl.when(r == source)
+    def _():
+        for d in range(1, 4):
+            cross(1, 1 - k, d).start()
+        own = pltpu.make_async_copy(g_ref.at[:, :, :, t], across_ref, local_sem.at[1])
+        own.start()
+        own.wait()
+        for d in range(1, 4):
+            cross(0, k, d).wait_send()
+            cross(1, 1 - k, d).wait_send()
+
+    @pl.when(r != source)
+    def _():
+        cross(0, k, 1).wait_recv()
+        cross(1, 1 - k, 1).wait_recv()
+
+
+def rows_call(mine):
+    lead, slab, n = mine.shape
+    return pl.pallas_call(
+        rows_body,
+        out_shape=[
+            jax.ShapeDtypeStruct((4, 4, 2, lead, slab, n), jnp.float32),
+            jax.ShapeDtypeStruct((4, 4, 2, slab, n), jnp.float32),
+        ],
+        in_specs=[pl.BlockSpec(memory_space=pl.ANY)],
+        out_specs=[pl.BlockSpec(memory_space=pl.ANY)] * 2,
+        scratch_shapes=gather_sems()
+        + [pltpu.SemaphoreType.DMA((2,)), pltpu.SemaphoreType.DMA((2, 4)), pltpu.SemaphoreType.DMA((2,))],
+        compiler_params=pltpu.CompilerParams(collective_id=1, has_side_effects=True, vmem_limit_bytes=56 * MIB),
+        cost_estimate=pl.CostEstimate(flops=0, bytes_accessed=1000, transcendentals=0),
+    )(mine)
+
+
+def panel_body(message_ref, own_ref, diag_ref, got_ref, share, front, units, packed, msg_send, msg_recv, local_sem,
+               f_send, f_recv, u_send, u_recv, send, recv, core_send, core_recv):
+    r, c, y, z, k = here()
+    n_col = got_ref.shape[0]
+    slab = got_ref.shape[1]
+    lead = share.shape[1]
+    half = units.shape[3]
+    greet([(r, lax.rem(c + d, n_col)) for d in range(1, n_col)] + row_peers(r, c))
+
+    def message(d):
+        to = lax.rem(c + d, n_col)
+        return pltpu.make_async_remote_copy(
+            src_ref=message_ref.at[to],
+            dst_ref=got_ref.at[c],
+            send_sem=msg_send.at[d],
+            recv_sem=msg_recv.at[d],
+            device_id=(r, to),
+            device_id_type=MESH,
+        )
+
+    keep = pltpu.make_async_copy(message_ref.at[c], got_ref.at[c], local_sem.at[0])
+    keep.start()
+    for d in range(1, n_col):
+        message(d).start()
+    keep.wait()
+    for d in range(1, n_col):
+        message(d).wait_recv()
+
+    def exchange(src, dst, s_sem, r_sem, d):
+        return pltpu.make_async_remote_copy(
+            src_ref=src, dst_ref=dst, send_sem=s_sem.at[d], recv_sem=r_sem.at[d], device_id=(turn(r, d), c),
+            device_id_type=MESH,
+        )
+
+    for q in range(4):
+        for t in range(lead):
+            share[q, t] = got_ref[4 * t + q, :, 4 * TILE:5 * TILE]
+    front[r] = share[r]
+    shares = [exchange(share.at[turn(r, d)], front.at[r], f_send, f_recv, d) for d in range(1, 4)]
+    for copy in shares:
+        copy.start()
+    own_ref[...] = jnp.zeros_like(own_ref)
+
+    def add(s, carry):
+        for q in range(4):
+            at = slice(q * TILE, (q + 1) * TILE)
+            label = got_ref[s, q:q + 1, 5 * TILE:5 * TILE + 128]
+            label = jnp.broadcast_to(jnp.concatenate([label, label], axis=1), (slab, TILE))
+            part = got_ref[s, :, at]
+            for t in range(lead):
+                rows = slice(t * slab, (t + 1) * slab)
+                own_ref[rows, at] = own_ref[rows, at] + jnp.where(label == float(t), part, 0.0)
+        return carry
+
+    lax.fori_loop(0, n_col, add, 0)
+    for copy in shares:
+        copy.wait_recv()
+    for q in range(4):
+        at = slice(q * TILE, (q + 1) * TILE)
+        for t in range(lead):
+            rows = slice(t * slab, (t + 1) * slab)
+            own_ref[rows, at] = own_ref[rows, at] + front[q, t]
+    for p in range(2):
+        units[r, p] = own_ref[:slab, p * half:(p + 1) * half]
+    lines = [exchange(units.at[r], units.at[r], u_send, u_recv, d) for d in range(1, 4)]
+    for copy in lines:
+        copy.start()
+    for copy in lines:
+        copy.wait_recv()
+    for q in range(4):
+        packed[q] = units[q, 0]
+    for q in range(2):
+        packed[4 + q] = units[2 + q, 1]
+    diag_ref[y, z, k] = packed[...]
+
+    def piece(h, yy, zz, kk):
+        return diag_ref.at[yy, zz, kk, pl.ds(h * 3, 3)]
+
+    finish = plane_gather(piece, send, recv, core_send, core_recv, r, y, z, k)
+    for d in range(1, n_col):
+        message(d).wait_send()
+    for copy in shares + lines:
+        copy.wait_send()
+    finish()
+
+
+def panel_call(message, lead):
+    n_col, slab, width = message.shape
+    half = 2 * TILE
+    dma = pltpu.SemaphoreType.DMA
+    vmem = pl.BlockSpec(memory_space=pltpu.VMEM)
+    return pl.pallas_call(
+        panel_body,
+        out_shape=[
+            jax.ShapeDtypeStruct((lead * slab, 4 * TILE), jnp.float32),
+            jax.ShapeDtypeStruct((4, 4, 2, 6, slab, half), jnp.float32),
+            jax.ShapeDtypeStruct((n_col, slab, width), jnp.float32),
+        ],
+        in_specs=[vmem],
+        out_specs=[vmem] * 3,
+        scratch_shapes=[
+            pltpu.VMEM((4, lead, slab, TILE), jnp.float32),
+            pltpu.VMEM((4, lead, slab, TILE), jnp.float32),
+            pltpu.VMEM((4, 2, slab, half), jnp.float32),
+            pltpu.VMEM((6, slab, half), jnp.float32),
+            dma((n_col,)),
+            dma((n_col,)),
+            dma((1,)),
+            dma((4,)),
+            dma((4,)),
+            dma((4,)),
+            dma((4,)),
+        ]
+        + gather_sems(),
+        compiler_params=pltpu.CompilerParams(collective_id=0, has_side_effects=True, vmem_limit_bytes=56 * MIB),
+        cost_estimate=pl.CostEstimate(flops=0, bytes_accessed=1000, transcendentals=0),
+    )(message)
 
 
 def pack_body(slot_ref, tile_ref, out_ref):
@@ -121,31 +416,6 @@
         ),
         cost_estimate=pl.CostEstimate(flops=0, bytes_accessed=n * t * t * 8, transcendentals=0),
     )(slots, tiles)
-
-
-def panel_body(got_ref, front_ref, out_ref):
-    sources, slab, _ = got_ref.shape
-    lead = front_ref.shape[1]
-    for q in range(4):
-        at = slice(q * TILE, (q + 1) * TILE)
-        acc = [front_ref[q, t] for t in range(lead)]
-        for s in range(sources):
-            label = got_ref[s, q:q + 1, 5 * TILE:5 * TILE + 128]
-            label = jnp.broadcast_to(jnp.concatenate([label, label], axis=1), (slab, TILE))
-            part = got_ref[s, :, at]
-            for t in range(lead):
-                acc[t] = acc[t] + jnp.where(label == float(t), part, 0.0)
-        for t in range(lead):
-            out_ref[t * slab:(t + 1) * slab, at] = acc[t]
-
-
-def panel_call(got, front_part):
-    lead, slab = front_part.shape[1], front_part.shape[2]
-    return pl.pallas_call(
-        panel_body,
-        out_shape=jax.ShapeDtypeStruct((lead * slab, 4 * TILE), jnp.float32),
-        cost_estimate=pl.CostEstimate(flops=0, bytes_accessed=got.size * 4, transcendentals=0),
-    )(got, front_part)
 
 
 def add_body(label_ref, front_ref, got_ref, out_ref):
@@ -230,7 +500,7 @@
             ],
             out_specs=pl.BlockSpec((1, TILE, TILE), lambda i, _: (i, 0, 0)),
         ),
-        compiler_params=pltpu.CompilerParams(vmem_limit_bytes=32 * MIB),
+        compiler_params=pltpu.CompilerParams(vmem_limit_bytes=56 * MIB),
         cost_estimate=pl.CostEstimate(flops=6 * lead * TILE * TILE * n, bytes_accessed=gathered.size * 4, transcendentals=0),
     )(col, acc, gathered, across)
 
@@ -262,23 +532,20 @@
     )
     marks = jnp.broadcast_to(marks[:, :, None], (n_col, slab, 128))
     message = jnp.concatenate([slabs, mirrored, marks], axis=2)
-    got = lax.all_to_all(message, "col", split_axis=0, concat_axis=0, tiled=True)
-    cross = got[:, :, 4 * TILE:5 * TILE].reshape(lead, n_row, slab, TILE).transpose(1, 0, 2, 3)
-    cross = lax.all_to_all(cross, "row", split_axis=0, concat_axis=0, tiled=True)
-    own = panel_call(got, cross)
+    own, parts, got = panel_call(message, lead)
 
     payload = pack_call(slot_of, tiles)
-    payload, got = lax.optimization_barrier((payload, got))
+    if LATE:
+        payload, own = lax.optimization_barrier((payload, own))
     arrived = lax.all_to_all(payload, "col", split_axis=0, concat_axis=0, tiled=True)
 
-    diag = lax.all_gather(own[:slab], ("row", "col"), axis=0, tiled=True)
     row_tiles = jnp.arange(lead, dtype=jnp.int32) * n_row + row_id
     keep = jnp.sum(jnp.where(row_tiles[:, None] == jnp.arange(tile_mask.shape[0])[None, :], tile_mask[None, :], 0), axis=1)
     where = jnp.concatenate([(row_id * TILE + col_id * slab)[None], keep[1:]]).astype(jnp.int32)
-    mine = chol_call(where, diag, own)
-    gathered = lax.all_gather(mine, "col", axis=0, tiled=False).reshape(n_col, lead, slab, 4 * TILE)
-    chosen = lax.dynamic_slice_in_dim(gathered, col_id // n_row, 1, axis=1).reshape(TILE, 4 * TILE)
-    across = lax.psum(jnp.where(row_id == col_id % n_row, chosen, 0.0), "row")
+    mine = chol_call(where, parts, own)
+    gathered, across = rows_call(mine.reshape(lead, slab, 4 * TILE))
+    gathered = gathered.reshape(n_col, lead, slab, 4 * TILE)
+    across = across.reshape(TILE, 4 * TILE)
 
     got_labels = got[:, 4, 5 * TILE].astype(jnp.int32)
     acc = add_call(got_labels, blocks, arrived)

time: 378 us -> 313 us (0.83)
  the two profiles are of different devices: /device:TPU:48 before, /device:TPU:52 now
where the time goes in v2:
time: 313 us; the launch traced here: 311 us
  Pallas kernels  287 us (92%)
  local copies, waits for them, and re-layouts  9.57 us (3%)
  starting transfers between devices  7.76 us (2%)
  other arithmetic  6.13 us (2%)
    pallas_call x1, Pallas kernels, rows_call(): pl.pallas_call(rows_body, out_shape=[jax.ShapeDtypeStruct((4, 4, 2, lead,...  142 us
    pallas_call x1, Pallas kernels, panel_call(): pl.pallas_call(panel_body, out_shape=[jax.ShapeDtypeStruct((lead * slab,...  57.1 us
    pallas_call x1, Pallas kernels, chol_call(): pl.pallas_call(chol_body, out_shape=jax.ShapeDtypeStruct((m, n), jnp.floa...  44.1 us
    pallas_call x2, Pallas kernels, pack_call(): pl.pallas_call(pack_body, out_shape=jax.ShapeDtypeStruct((n, t, t), tiles...  23.9 us
    pallas_call x1, Pallas kernels, add_call(): pl.pallas_call(add_body, out_shape=jax.ShapeDtypeStruct(front.shape, jnp....  9.9 us
    pallas_call x1, Pallas kernels, final_call(): pl.pallas_call(final_body, out_shape=jax.ShapeDtypeStruct(acc.shape, jnp....  9.79 us
    all_to_all x1, starting transfers between devices, local(): lax.all_to_all(payload, 'col', split_axis=0, concat_axis=0, tiled=True)  7.76 us
  transfers between devices with their start and end apart: 1, of which 0 were waited for; matrix products, arithmetic and copies ran while one was open for 1% of the time, Pallas kernels for 60%

profile of v2, /device:TPU:52, one launch (start us, length us, event | category | flops | bytes accessed | tf_op | source)
XLA Modules:
  0.0 311.3 jit_solution(16177549063417002595)
XLA Ops:
  0.7 0.7 add_bitcast_fusion
  1.3 1.3 select_reduce_fusion.1
  2.6 0.1 pad.7.clone
  2.7 0.1 maximum_maximum_fusion
  2.7 0.1 copy.21
  2.8 1.1 slice.17
  4.0 0.1 copy.25
  4.1 19.9 %shard_map.66 = f32[32,256,256]{2,1,0:T(8,128)} custom-call(s32[32]{0:T(128)} %get-tuple-element.19.slot_ref, f32[32,256,256]{2,1,0:T(8,128)} %bitcast.29), custom_call_target="tpu_custom_call" | custom-call | bytes 16777216 | tf_op jit(solution)/shard_map/pallas_call | solution.py:408
  24.0 4.0 %shard_map.64 = f32[4,256,256]{2,1,0:T(8,128)} custom-call(s32[4]{0:T(128)} %bitcast.39, f32[32,256,256]{2,1,0:T(8,128)} %bitcast.30), custom_call_target="tpu_custom_call" | custom-call | bytes 2097152 | tf_op jit(solution)/shard_map/pallas_call | solution.py:408
  28.0 1.3 copy.19
  29.4 0.1 broadcast_in_dim.60
  29.5 1.2 pad_maximum_fusion.message_ref
  30.7 57.1 %shard_map.65 = (f32[64,1024]{1,0:T(8,128)}, f32[4,4,2,6,8,512]{5,4,3,2,1,0:T(8,128)}, f32[32,8,1408]{2,1,0:T(8,128)}) custom-call(f32[32,8,1408]{2,1,0:T(8,128)} %pad_maximum_fusion.message_ref), custom_call_target="tpu_custom_call" | custom-call | bytes 1000 | tf_op jit(solution)/shard_map/pallas_call | solution.py:373
  87.8 0.0 copy-start
  87.8 7.8 %all-to-all-start = ((f32[32,256,256]{2,1,0:T(8,128)}), f32[32,256,256]{2,1,0:T(8,128)}, u32[]{:S(2)}, u32[]{:S(2)}) async-start(f32[32,256,256]{2,1,0:T(8,128)} %shard_map.66), calls=%async_computation | async-start | bytes 16777216 | tf_op jit(solution)/shard_map/all_to_all | solution.py:540
  95.6 0.0 copy-done
  95.6 0.0 copy-start.1
  95.6 1.5 copy.27
  97.2 0.0 copy-done.1
  97.2 0.2 select_reduce_fusion.2
  97.3 0.1 slice.20
  97.4 0.6 pad_add_fusion.where_ref
  98.0 44.1 %shard_map.68 = f32[64,1024]{1,0:T(8,128)} custom-call(s32[8]{0:T(128)} %pad_add_fusion.where_ref, f32[4,4,2,6,8,512]{5,4,3,2,1,0:T(8,128)} %get-tuple-element.15.part_ref, f32[64,1024]{1,0:T(8,128)} %get-tuple-element.16.own_ref), custom_call_target="tpu_custom_call" | custom-call | bytes 1000 | tf_op jit(solution)/shard_map/pallas_call | solution.py:102
  142.1 142.3 %shard_map.69 = (f32[4,4,2,8,8,1024]{5,4,3,2,1,0:T(8,128)}, f32[4,4,2,8,1024]{4,3,2,1,0:T(8,128)}) custom-call(f32[8,8,1024]{2,1,0:T(8,128)} %bitcast.37), custom_call_target="tpu_custom_call" | custom-call | bytes 1000 | tf_op jit(solution)/shard_map/pallas_call | solution.py:267
  284.4 2.1 convert_reduce_fusion.label_ref
  286.6 0.0 all-to-all-done.got_ref
  286.6 9.9 %shard_map.67.acc_ref = f32[8,256,256]{2,1,0:T(8,128)} custom-call(s32[32]{0:T(128)} %convert_reduce_fusion.label_ref, f32[8,256,256]{2,1,0:T(8,128)} %bitcast.31, f32[32,256,256]{2,1,0:T(8,128)} %all-to-all-done.got_ref), custom_call_target="tpu_custom_call" | custom-call | bytes 12582912 | tf_op jit(solution)/shard_map/pallas_call | solution.py:440
  296.5 9.8 %shard_map.70 = f32[8,256,256]{2,1,0:T(8,128)} custom-call(s32[1]{0:T(128)} %bitcast.col_ref, f32[8,256,256]{2,1,0:T(8,128)} %shard_map.67.acc_ref, f32[32,8,8,1024]{3,2,1,0:T(8,128)} %bitcast.32, f32[256,1024]{1,0:T(8,128)} %bitcast.38), custom_call_target="tpu_custom_call" | custom-call | flops 3221225472 | bytes 8388608 | tf_op jit(solution)/shard_map/pallas_call | solution.py:490
  306.3 5.1 %copy.22 = f32[8,1,256,1,1,256]{5,4,3,2,1,0:T(1,128)} copy(f32[8,1,256,1,1,256]{5,2,0,4,3,1:T(8,128)} %bitcast.33) | data formatting | bytes 4194304 | tf_op jit(solution)/shard_map/reshape | solution.py:553
  (5 shorter events, 0.0 us)
Async XLA Ops:
  87.8 7.8 %copy-start = (f32[8,1,256,1,1,256]{5,4,3,2,1,0:T(1,128)S(1)}, f32[8,1,256,1,1,256]{5,4,3,2,1,0:T(1,128)}, u32[]{:S(2)}) copy-start(f32[8,1,256,1,1,256]{5,4,3,2,1,0:T(1,128)} %param.6) | copy-start | bytes 6291460
  87.8 198.7 %all-to-all-start = ((f32[32,256,256]{2,1,0:T(8,128)}), f32[32,256,256]{2,1,0:T(8,128)}, u32[]{:S(2)}, u32[]{:S(2)}) async-start(f32[32,256,256]{2,1,0:T(8,128)} %shard_map.66), calls=%async_computation | async-start | bytes 16777216 | tf_op jit(solution)/shard_map/all_to_all | solution.py:540
  95.6 1.6 copy-start.1

commit v3 on v2

--- a/solution.py
+++ b/solution.py
@@ -10,7 +10,6 @@
 SB = 32
 TILE = 256
 MIB = 1024 * 1024
-LATE = True
 
 def dot_nt(a, b):
     return lax.dot_general(a, b, (((1,), (1,)), ((), ())), precision=HI, preferred_element_type=jnp.float32)
@@ -57,14 +56,14 @@
             rest = rest[SB:] - dot_tn(r[:, lo:NB], r)
     return jnp.concatenate(done, axis=0)
 
-def chol_body(where_ref, part_ref, own_ref, out_ref, s, diag_ref):
+def load_diag(part_ref, own_ref, where_ref, diag_ref, s):
     n = diag_ref.shape[0]
+    m = own_ref.shape[0]
     for q in range(4):
         rows = slice(q * TILE, (q + 1) * TILE)
         diag_ref[rows, :2 * TILE] = part_ref[:, :, :, q].reshape(TILE, 2 * TILE)
         if q >= 2:
             diag_ref[rows, 2 * TILE:] = part_ref[:, :, :, 2 + q].reshape(TILE, 2 * TILE)
-    m = own_ref.shape[0]
     nb = n // NB
     half = nb // 2
     for a in range(nb):
@@ -76,38 +75,35 @@
             s[a * NB:(a + 1) * NB, b * NB:(b + 1) * NB] = x
         if a + 1 < nb:
             s[a * NB:(a + 1) * NB, (a + 1) * NB:] = jnp.zeros((NB, n - (a + 1) * NB), jnp.float32)
-    row0 = where_ref[0]
+    row0 = lax.axis_index("row") * TILE + lax.axis_index("col") * 8
     s[n:n + 8, :] = s[pl.ds(pl.multiple_of(row0, 8), 8), :]
     for t in range(1, m // 8):
-        s[n + 8 * t:n + 8 * t + 8, :] = jnp.where(where_ref[t] > 0, own_ref[8 * t:8 * t + 8, :], 0.0)
-    for k in range(nb):
-        lo = k * NB
-        hi = lo + NB
-        inv = invert_factor(s[lo:hi, lo:hi])
-        x = dot_nt(s[hi:, lo:hi], inv)
-        s[hi:, lo:hi] = x
-        at = hi
-        while at < n:
-            width = NB if at == hi else min(2 * NB, n - at)
-            s[at:, at:at + width] = s[at:, at:at + width] - dot_nt(x[at - hi:], x[at - hi:at - hi + width])
-            at += width
-    res = s[n:, :]
-    ids = lax.broadcasted_iota(jnp.int32, (m, n), 0)
-    lane = lax.broadcasted_iota(jnp.int32, (m, n), 1)
-    out_ref[...] = jnp.where((ids >= 8) | (lane <= ids + row0), res, 0.0)
-
-def chol_call(where, parts, own):
-    m, n = own.shape
-    vmem = pl.BlockSpec(memory_space=pltpu.VMEM)
-    return pl.pallas_call(
-        chol_body,
-        out_shape=jax.ShapeDtypeStruct((m, n), jnp.float32),
-        in_specs=[pl.BlockSpec(memory_space=pltpu.SMEM), vmem, vmem],
-        out_specs=vmem,
-        scratch_shapes=[pltpu.VMEM((n + m, n), jnp.float32), pltpu.VMEM((n, n), jnp.float32)],
-        compiler_params=pltpu.CompilerParams(vmem_limit_bytes=56 * MIB),
-        cost_estimate=pl.CostEstimate(flops=0, bytes_accessed=1000, transcendentals=0),
-    )(where, parts, own)
+        s[n + 8 * t:n + 8 * t + 8, :] = jnp.where(where_ref[t:t + 1, :1] > 0.0, own_ref[8 * t:8 * t + 8, :], 0.0)
+    return row0
+
+
+def factor_step(s, k):
+    n = s.shape[1]
+    lo = k * NB
+    hi = lo + NB
+    inv = invert_factor(s[lo:hi, lo:hi])
+    x = dot_nt(s[hi:, lo:hi], inv)
+    s[hi:, lo:hi] = x
+    at = hi
+    while at < n:
+        width = NB if at == hi else min(2 * NB, n - at)
+        s[at:, at:at + width] = s[at:, at:at + width] - dot_nt(x[at - hi:], x[at - hi:at - hi + width])
+        at += width
+
+
+def split(x):
+    high = x.astype(jnp.bfloat16)
+    low = (x - high.astype(jnp.float32)).astype(jnp.bfloat16)
+    return high, low
+
+
+def nt(a, b):
+    return lax.dot_general(a, b, (((1,), (1,)), ((), ())), preferred_element_type=jnp.float32)
 
 
 MESH = pl.DeviceIdType.MESH
@@ -146,7 +142,7 @@
     return [(turn(r, d), c) for d in range(1, 4)]
 
 
-def plane_gather(piece, send, recv, core_send, core_recv, r, y, z, k):
+def plane_gather(piece, send, recv, core_send, core_recv, r, y, z, k, early=None, done=None):
     def place(h, a, b):
         return (b, a) if h == 0 else (a, b)
 
@@ -184,6 +180,8 @@
             second[h, 0, d] = along_second(h, 0, d)
     for h in range(2):
         core[h, 0, 0] = across(h, 0, 0)
+    if early is not None:
+        early()
     for da in range(1, 4):
         for h in range(2):
             first[h, da].wait_recv()
@@ -195,10 +193,16 @@
             for h in range(2):
                 second[h, da, db].wait_recv()
                 core[h, da, db] = across(h, da, db)
+        if done is not None:
+            done(da, 0)
 
     def finish():
-        for copy in core.values():
-            copy.wait_recv()
+        for da in range(4):
+            for h in range(2):
+                for db in range(4):
+                    core[h, da, db].wait_recv()
+            if done is not None:
+                done(da, 1)
         for group in (first, second, core):
             for copy in group.values():
                 copy.wait_send()
@@ -210,76 +214,7 @@
     return [pltpu.SemaphoreType.DMA((2, 4, 4)) for _ in range(4)]
 
 
-def rows_body(mine_ref, g_ref, across_ref, send, recv, core_send, core_recv, local_sem, x_send, x_recv):
-    r, c, y, z, k = here()
-    greet(plane_peers(r, y, z, k) + row_peers(r, c))
-    keep = pltpu.make_async_copy(mine_ref, g_ref.at[y, z, k], local_sem.at[0])
-    keep.start()
-    keep.wait()
-    half = mine_ref.shape[0] // 2
-
-    def piece(h, yy, zz, kk):
-        return g_ref.at[yy, zz, kk, pl.ds(h * half, half)]
-
-    finish = plane_gather(piece, send, recv, core_send, core_recv, r, y, z, k)
-    t = lax.div(c, 4)
-    source = lax.rem(c, 4)
-
-    def slab(kk):
-        return g_ref.at[:, :, kk, t]
-
-    def cross(i, kk, d):
-        return pltpu.make_async_remote_copy(
-            src_ref=slab(kk),
-            dst_ref=across_ref.at[:, :, kk],
-            send_sem=x_send.at[i, d],
-            recv_sem=x_recv.at[i],
-            device_id=(turn(r, d), c),
-            device_id_type=MESH,
-        )
-
-    @pl.when(r == source)
-    def _():
-        for d in range(1, 4):
-            cross(0, k, d).start()
-
-    finish()
-
-    @pl.when(r == source)
-    def _():
-        for d in range(1, 4):
-            cross(1, 1 - k, d).start()
-        own = pltpu.make_async_copy(g_ref.at[:, :, :, t], across_ref, local_sem.at[1])
-        own.start()
-        own.wait()
-        for d in range(1, 4):
-            cross(0, k, d).wait_send()
-            cross(1, 1 - k, d).wait_send()
-
-    @pl.when(r != source)
-    def _():
-        cross(0, k, 1).wait_recv()
-        cross(1, 1 - k, 1).wait_recv()
-
-
-def rows_call(mine):
-    lead, slab, n = mine.shape
-    return pl.pallas_call(
-        rows_body,
-        out_shape=[
-            jax.ShapeDtypeStruct((4, 4, 2, lead, slab, n), jnp.float32),
-            jax.ShapeDtypeStruct((4, 4, 2, slab, n), jnp.float32),
-        ],
-        in_specs=[pl.BlockSpec(memory_space=pl.ANY)],
-        out_specs=[pl.BlockSpec(memory_space=pl.ANY)] * 2,
-        scratch_shapes=gather_sems()
-        + [pltpu.SemaphoreType.DMA((2,)), pltpu.SemaphoreType.DMA((2, 4)), pltpu.SemaphoreType.DMA((2,))],
-        compiler_params=pltpu.CompilerParams(collective_id=1, has_side_effects=True, vmem_limit_bytes=56 * MIB),
-        cost_estimate=pl.CostEstimate(flops=0, bytes_accessed=1000, transcendentals=0),
-    )(mine)
-
-
-def panel_body(message_ref, own_ref, diag_ref, got_ref, share, front, units, packed, msg_send, msg_recv, local_sem,
+def panel_body(message_ref, own_ref, diag_ref, label_ref, got_ref, share, front, units, packed, msg_send, msg_recv, local_sem,
                f_send, f_recv, u_send, u_recv, send, recv, core_send, core_recv):
     r, c, y, z, k = here()
     n_col = got_ref.shape[0]
@@ -320,6 +255,7 @@
     shares = [exchange(share.at[turn(r, d)], front.at[r], f_send, f_recv, d) for d in range(1, 4)]
     for copy in shares:
         copy.start()
+    label_ref[...] = got_ref[:, 4, 5 * TILE:5 * TILE + 128]
     own_ref[...] = jnp.zeros_like(own_ref)
 
     def add(s, carry):
@@ -375,11 +311,12 @@
         out_shape=[
             jax.ShapeDtypeStruct((lead * slab, 4 * TILE), jnp.float32),
             jax.ShapeDtypeStruct((4, 4, 2, 6, slab, half), jnp.float32),
-            jax.ShapeDtypeStruct((n_col, slab, width), jnp.float32),
+            jax.ShapeDtypeStruct((n_col, 128), jnp.float32),
         ],
         in_specs=[vmem],
         out_specs=[vmem] * 3,
         scratch_shapes=[
+            pltpu.VMEM((n_col, slab, width), jnp.float32),
             pltpu.VMEM((4, lead, slab, TILE), jnp.float32),
             pltpu.VMEM((4, lead, slab, TILE), jnp.float32),
             pltpu.VMEM((4, 2, slab, half), jnp.float32),
@@ -398,6 +335,205 @@
     )(message)
 
 
+def main_body(keep_ref, label_ref, parts_ref, own_ref, front_ref, payload_ref, out_ref, s, diag, g, across, arrived, high, low,
+              a_send, a_recv, local_sem, x_send, x_recv, send, recv, core_send, core_recv):
+    r, c, y, z, k = here()
+    n_col = arrived.shape[0]
+    lead = front_ref.shape[0]
+    n = s.shape[1]
+    greet([(r, lax.rem(c + d, n_col)) for d in range(1, n_col)] + row_peers(r, c))
+
+    def tile(d):
+        to = lax.rem(c + d, n_col)
+        return pltpu.make_async_remote_copy(
+            src_ref=payload_ref.at[to],
+            dst_ref=arrived.at[d],
+            send_sem=a_send.at[d],
+            recv_sem=a_recv.at[d],
+            device_id=(r, to),
+            device_id_type=MESH,
+        )
+
+    def begin(ds):
+        for d in ds:
+            @pl.when(lax.rem(c + d, n_col) >= 4)
+            def _(d=d):
+                tile(d).start()
+
+    own_tile = pltpu.make_async_copy(payload_ref.at[c], arrived.at[0], local_sem.at[0])
+    own_tile.start()
+    order = list(range(1, n_col))
+    plan = [3, 2, 2, 2, 2, 2, 2, 1]
+    groups = []
+    for size in plan:
+        groups.append(order[:size])
+        order = order[size:]
+    row0 = None
+    begin(groups[0])
+    row0 = load_diag(parts_ref, own_ref, keep_ref, diag, s)
+    for t in range(lead):
+        out_ref[t] = front_ref[t]
+    for step in range(n // NB):
+        if step:
+            begin(groups[step])
+        factor_step(s, step)
+    m = s.shape[0] - n
+    ids = lax.broadcasted_iota(jnp.int32, (m, n), 0)
+    lane = lax.broadcasted_iota(jnp.int32, (m, n), 1)
+    mine = jnp.where((ids >= 8) | (lane <= ids + row0), s[n:, :], 0.0)
+    g[y, z, k] = mine.reshape(g.shape[3:])
+
+    half = lead // 2
+
+    def piece(h, yy, zz, kk):
+        return g.at[yy, zz, kk, pl.ds(h * half, half)]
+
+    t_of = lax.div(c, 4)
+    source = lax.rem(c, 4)
+    part = lax.div(t_of, half)
+
+    def cross(h, da, mate, d):
+        kk = lax.rem(k + mate, 2)
+        if h == 0:
+            zz = turn(z, 4 - da)
+            src, dst = g.at[:, zz, kk, t_of], across.at[:, zz, kk]
+        else:
+            yy = turn(y, 4 - da)
+            src, dst = g.at[yy, :, kk, t_of], across.at[yy, :, kk]
+        return pltpu.make_async_remote_copy(
+            src_ref=src, dst_ref=dst, send_sem=x_send.at[mate, da, d], recv_sem=x_recv.at[mate, da],
+            device_id=(turn(r, d), c), device_id_type=MESH,
+        )
+
+    def forward(da, mate):
+        for h in range(2):
+            @pl.when((r == source) & (part == h))
+            def _(h=h):
+                for d in range(1, 4):
+                    cross(h, da, mate, d).start()
+
+    later = order
+
+    def early():
+        begin(later[:4])
+
+    finish = plane_gather(piece, send, recv, core_send, core_recv, r, y, z, k, early, forward)
+    begin(later[4:])
+
+    def absorb(ds):
+        @pl.when(c >= 4)
+        def _():
+            for d in ds:
+                if d:
+                    tile(d).wait_recv()
+            wanted = [
+                jnp.concatenate([label_ref[pl.ds(lax.rem(c + n_col - d, n_col), 1), :]] * 2, axis=1) for d in ds
+            ]
+
+            def strip(i, carry):
+                rows = pl.ds(pl.multiple_of(i * 8, 8), 8)
+                acc = [out_ref[t, rows, :] for t in range(lead)]
+                for d, want in zip(ds, wanted):
+                    part_in = arrived[d, rows, :]
+                    want = jnp.broadcast_to(want, (8, TILE))
+                    for t in range(lead):
+                        acc[t] = acc[t] + jnp.where(want == float(t), part_in, 0.0)
+                for t in range(lead):
+                    out_ref[t, rows, :] = acc[t]
+                return carry
+
+            lax.fori_loop(0, TILE // 8, strip, 0)
+
+    own_tile.wait()
+    absorb([0] + sum(groups[:4], []))
+    finish()
+
+    @pl.when(r == source)
+    def _():
+        local_copy = pltpu.make_async_copy(g.at[:, :, :, t_of], across, local_sem.at[1])
+        local_copy.start()
+        local_copy.wait()
+
+    for h in range(2):
+        @pl.when((r != source) & (part == h))
+        def _(h=h):
+            for mate in range(2):
+                for da in range(4):
+                    cross(h, da, mate, 1).wait_recv()
+
+    @pl.when(c < 4)
+    def _():
+        at = pl.multiple_of(jnp.minimum(c, 3) * TILE, TILE)
+        for t in range(lead):
+            out_ref[t] = g[:, :, :, t, :, pl.ds(at, TILE)].reshape(TILE, TILE)
+
+    @pl.when(c >= 4)
+    def _():
+        high[...], low[...] = split(across[...].reshape(TILE, n))
+
+        def update(t, carry):
+            ah, al = split(g[:, :, :, t].reshape(TILE, n))
+            out_ref[t] = out_ref[t] - (nt(ah, high[...]) + (nt(ah, low[...]) + nt(al, high[...])))
+            return carry
+
+        lax.fori_loop(1, lead, update, 0)
+
+    absorb(sum(groups[4:], []))
+    rest = list(later)
+    while rest:
+        size = 4 if len(rest) > 6 else 2
+        absorb(rest[:size])
+        rest = rest[size:]
+
+    @pl.when(c >= 4)
+    def _():
+        out_ref[0] = jnp.zeros((TILE, TILE), jnp.float32)
+
+    for d in range(1, n_col):
+        @pl.when(lax.rem(c + d, n_col) >= 4)
+        def _(d=d):
+            tile(d).wait_send()
+
+    for h in range(2):
+        @pl.when((r == source) & (part == h))
+        def _(h=h):
+            for mate in range(2):
+                for da in range(4):
+                    for d in range(1, 4):
+                        cross(h, da, mate, d).wait_send()
+
+
+def main_call(keep, labels, parts, own, blocks, payload):
+    lead = blocks.shape[0]
+    n_col = payload.shape[0]
+    m, n = own.shape
+    dma = pltpu.SemaphoreType.DMA
+    vmem = pl.BlockSpec(memory_space=pltpu.VMEM)
+    return pl.pallas_call(
+        main_body,
+        out_shape=jax.ShapeDtypeStruct(blocks.shape, jnp.float32),
+        in_specs=[vmem] * 5 + [pl.BlockSpec(memory_space=pl.ANY)],
+        out_specs=vmem,
+        scratch_shapes=[
+            pltpu.VMEM((n + m, n), jnp.float32),
+            pltpu.VMEM((n, n), jnp.float32),
+            pltpu.VMEM((4, 4, 2, lead, m // lead, n), jnp.float32),
+            pltpu.VMEM((4, 4, 2, m // lead, n), jnp.float32),
+            pltpu.VMEM((n_col, TILE, TILE), jnp.float32),
+            pltpu.VMEM((TILE, n), jnp.bfloat16),
+            pltpu.VMEM((TILE, n), jnp.bfloat16),
+            dma((n_col,)),
+            dma((n_col,)),
+            dma((2,)),
+            dma((2, 4, 4)),
+            dma((2, 4)),
+        ]
+        + gather_sems(),
+        compiler_params=pltpu.CompilerParams(collective_id=1, has_side_effects=True, vmem_limit_bytes=58 * MIB),
+        cost_estimate=pl.CostEstimate(flops=0, bytes_accessed=1000, transcendentals=0),
+    )(keep, labels, parts, own, blocks, payload)
+
+
 def pack_body(slot_ref, tile_ref, out_ref):
     out_ref[...] = tile_ref[...]
 
@@ -416,93 +552,6 @@
         ),
         cost_estimate=pl.CostEstimate(flops=0, bytes_accessed=n * t * t * 8, transcendentals=0),
     )(slots, tiles)
-
-
-def add_body(label_ref, front_ref, got_ref, out_ref):
-    out_ref[...] = front_ref[...]
-
-    def step(s, carry):
-        p = label_ref[s]
-
-        @pl.when(p >= 0)
-        def _():
-            out_ref[p] = out_ref[p] + got_ref[s]
-
-        return carry
-
-    lax.fori_loop(0, got_ref.shape[0], step, 0)
-
-
-def add_call(labels, front, got):
-    lead = front.shape[0]
-    n = got.shape[0]
-    rows = 32
-    return pl.pallas_call(
-        add_body,
-        out_shape=jax.ShapeDtypeStruct(front.shape, jnp.float32),
-        grid_spec=pltpu.PrefetchScalarGridSpec(
-            num_scalar_prefetch=1,
-            grid=(TILE // rows,),
-            in_specs=[
-                pl.BlockSpec((lead, rows, TILE), lambda i, _: (0, i, 0)),
-                pl.BlockSpec((n, rows, TILE), lambda i, _: (0, i, 0)),
-            ],
-            out_specs=pl.BlockSpec((lead, rows, TILE), lambda i, _: (0, i, 0)),
-        ),
-        cost_estimate=pl.CostEstimate(flops=0, bytes_accessed=(n + 2 * lead) * TILE * TILE * 4, transcendentals=0),
-    )(labels, front, got)
-
-
-def split(x):
-    high = x.astype(jnp.bfloat16)
-    low = (x - high.astype(jnp.float32)).astype(jnp.bfloat16)
-    return high, low
-
-
-def nt(a, b):
-    return lax.dot_general(a, b, (((1,), (1,)), ((), ())), preferred_element_type=jnp.float32)
-
-
-def final_body(col_ref, acc_ref, l_ref, across_ref, out_ref):
-    c = col_ref[0]
-    t = pl.program_id(0)
-    n = across_ref.shape[1]
-
-    @pl.when(c < 4)
-    def _():
-        at = pl.multiple_of(jnp.minimum(c, 3) * TILE, TILE)
-        out_ref[0] = l_ref[:, 0, :, pl.ds(at, TILE)].reshape(TILE, TILE)
-
-    @pl.when((c >= 4) & (t == 0))
-    def _():
-        out_ref[...] = jnp.zeros_like(out_ref)
-
-    @pl.when((c >= 4) & (t > 0))
-    def _():
-        ah, al = split(l_ref[...].reshape(TILE, n))
-        bh, bl = split(across_ref[...])
-        out_ref[0] = acc_ref[0] - (nt(ah, bh) + (nt(ah, bl) + nt(al, bh)))
-
-
-def final_call(col, acc, gathered, across):
-    lead = acc.shape[0]
-    j, _, slab, n = gathered.shape
-    return pl.pallas_call(
-        final_body,
-        out_shape=jax.ShapeDtypeStruct(acc.shape, jnp.float32),
-        grid_spec=pltpu.PrefetchScalarGridSpec(
-            num_scalar_prefetch=1,
-            grid=(lead,),
-            in_specs=[
-                pl.BlockSpec((1, TILE, TILE), lambda i, _: (i, 0, 0)),
-                pl.BlockSpec((j, 1, slab, n), lambda i, _: (0, i, 0, 0)),
-                pl.BlockSpec((TILE, n), lambda i, _: (0, 0)),
-            ],
-            out_specs=pl.BlockSpec((1, TILE, TILE), lambda i, _: (i, 0, 0)),
-        ),
-        compiler_params=pltpu.CompilerParams(vmem_limit_bytes=56 * MIB),
-        cost_estimate=pl.CostEstimate(flops=6 * lead * TILE * TILE * n, bytes_accessed=gathered.size * 4, transcendentals=0),
-    )(col, acc, gathered, across)
 
 
 def local(front, child_tiles, child_owner, child_place, child_count, tile_mask):
@@ -532,24 +581,12 @@
     )
     marks = jnp.broadcast_to(marks[:, :, None], (n_col, slab, 128))
     message = jnp.concatenate([slabs, mirrored, marks], axis=2)
-    own, parts, got = panel_call(message, lead)
-
+    own, parts, labels = panel_call(message, lead)
     payload = pack_call(slot_of, tiles)
-    if LATE:
-        payload, own = lax.optimization_barrier((payload, own))
-    arrived = lax.all_to_all(payload, "col", split_axis=0, concat_axis=0, tiled=True)
-
     row_tiles = jnp.arange(lead, dtype=jnp.int32) * n_row + row_id
     keep = jnp.sum(jnp.where(row_tiles[:, None] == jnp.arange(tile_mask.shape[0])[None, :], tile_mask[None, :], 0), axis=1)
-    where = jnp.concatenate([(row_id * TILE + col_id * slab)[None], keep[1:]]).astype(jnp.int32)
-    mine = chol_call(where, parts, own)
-    gathered, across = rows_call(mine.reshape(lead, slab, 4 * TILE))
-    gathered = gathered.reshape(n_col, lead, slab, 4 * TILE)
-    across = across.reshape(TILE, 4 * TILE)
-
-    got_labels = got[:, 4, 5 * TILE].astype(jnp.int32)
-    acc = add_call(got_labels, blocks, arrived)
-    result = final_call(col_id.reshape(1), acc, gathered, across)
+    keep = jnp.broadcast_to(keep.astype(jnp.float32)[:, None], (lead, 128))
+    result = main_call(keep, labels, parts, own, blocks, payload)
     return result.reshape(front.shape)
 
 

time: 313 us -> 301 us (0.962)
  the two profiles are of different devices: /device:TPU:52 before, /device:TPU:113 now
where the time goes in v3:
time: 301 us; the launch traced here: 300 us
  Pallas kernels  285 us (95%)
  local copies, waits for them, and re-layouts  10.1 us (3%)
  other arithmetic  4.12 us (1%)
    pallas_call x1, Pallas kernels, main_call(): pl.pallas_call(main_body, out_shape=jax.ShapeDtypeStruct(blocks.shape, jn...  204 us
    pallas_call x1, Pallas kernels, panel_call(): pl.pallas_call(panel_body, out_shape=[jax.ShapeDtypeStruct((lead * slab,...  56.9 us
    pallas_call x2, Pallas kernels, pack_call(): pl.pallas_call(pack_body, out_shape=jax.ShapeDtypeStruct((n, t, t), tiles...  23.9 us

profile of v3, /device:TPU:113, one launch (start us, length us, event | category | flops | bytes accessed | tf_op | source)
XLA Modules:
  0.0 299.7 jit_solution(9848765962636253125)
XLA Ops:
  0.7 0.8 select_reduce_fusion.2
  1.5 0.7 add_bitcast_fusion
  2.2 1.3 select_reduce_fusion.1
  3.5 0.1 pad.5.clone
  3.6 0.1 maximum_maximum_fusion
  3.7 0.7 broadcast_in_dim.60.keep_ref
  4.3 0.1 copy.17
  4.4 0.1 broadcast_in_dim.66
  4.5 1.1 slice.11
  5.6 0.1 copy.21
  5.8 4.0 %shard_map.64 = f32[4,256,256]{2,1,0:T(8,128)} custom-call(s32[4]{0:T(128)} %bitcast.31, f32[32,256,256]{2,1,0:T(8,128)} %bitcast.24), custom_call_target="tpu_custom_call" | custom-call | bytes 2097152 | tf_op jit(solution)/shard_map/pallas_call | solution.py:544
  9.8 1.3 copy.15
  11.2 0.0 copy-start
  11.2 1.2 pad_maximum_fusion.message_ref
  12.4 56.9 %shard_map.65 = (f32[64,1024]{1,0:T(8,128)}, f32[4,4,2,6,8,512]{5,4,3,2,1,0:T(8,128)}, f32[32,128]{1,0:T(8,128)}) custom-call(f32[32,8,1408]{2,1,0:T(8,128)} %pad_maximum_fusion.message_ref), custom_call_target="tpu_custom_call" | custom-call | bytes 1000 | tf_op jit(solution)/shard_map/pallas_call | solution.py:309
  69.3 0.0 copy-done
  69.3 1.5 copy.23
  70.8 19.9 %shard_map.66.payload_ref = f32[32,256,256]{2,1,0:T(8,128)} custom-call(s32[32]{0:T(128)} %get-tuple-element.11.slot_ref, f32[32,256,256]{2,1,0:T(8,128)} %bitcast.25), custom_call_target="tpu_custom_call" | custom-call | bytes 16777216 | tf_op jit(solution)/shard_map/pallas_call | solution.py:544
  90.7 204.0 %shard_map.67 = f32[8,256,256]{2,1,0:T(8,128)} custom-call(f32[8,128]{1,0:T(8,128)} %broadcast_in_dim.60.keep_ref, f32[32,128]{1,0:T(8,128)} %get-tuple-element.8.label_ref, f32[4,4,2,6,8,512]{5,4,3,2,1,0:T(8,128)} %get-tuple-element.9.parts_ref, f32[64,1024]{1,0:T(8,128)} %get-tuple-element.10.own_ref, f32[8,256,256]{2,1,0:T(8,128)} %bitcast.26, ...), custom_call_target="tpu_custom_call" | custom-call | bytes 1000 | tf_op jit(solution)/shard_map/pallas_call | solution.py:512
  294.6 5.1 %copy.18 = f32[8,1,256,1,1,256]{5,4,3,2,1,0:T(1,128)} copy(f32[8,1,256,1,1,256]{5,2,0,4,3,1:T(8,128)} %bitcast.27) | data formatting | bytes 4194304 | tf_op jit(solution)/shard_map/reshape | solution.py:590
  (6 shorter events, 0.0 us)
Async XLA Ops:
  11.2 58.1 %copy-start = (f32[8,1,256,1,1,256]{5,4,3,2,1,0:T(1,128)S(1)}, f32[8,1,256,1,1,256]{5,4,3,2,1,0:T(1,128)}, u32[]{:S(2)}) copy-start(f32[8,1,256,1,1,256]{5,4,3,2,1,0:T(1,128)} %param.6) | copy-start | bytes 6291460

commit v4 on v3

--- a/solution.py
+++ b/solution.py
@@ -56,29 +56,30 @@
             rest = rest[SB:] - dot_tn(r[:, lo:NB], r)
     return jnp.concatenate(done, axis=0)
 
-def load_diag(part_ref, own_ref, where_ref, diag_ref, s):
-    n = diag_ref.shape[0]
+def load_diag(part_ref, own_ref, keep_ref, s):
+    n = s.shape[1]
     m = own_ref.shape[0]
-    for q in range(4):
-        rows = slice(q * TILE, (q + 1) * TILE)
-        diag_ref[rows, :2 * TILE] = part_ref[:, :, :, q].reshape(TILE, 2 * TILE)
-        if q >= 2:
-            diag_ref[rows, 2 * TILE:] = part_ref[:, :, :, 2 + q].reshape(TILE, 2 * TILE)
     nb = n // NB
     half = nb // 2
+
+    def block(a, b):
+        unit = a // 2 + (2 if b >= half else 0)
+        at = b % half * NB
+        y = a % 2 * 2
+        return part_ref[y:y + 2, :, :, unit, :, at:at + NB].reshape(NB, NB)
+
     for a in range(nb):
         for b in range(a + 1):
-            x = diag_ref[a * NB:(a + 1) * NB, b * NB:(b + 1) * NB]
+            x = block(a, b)
             if a // half == b // half:
-                y = diag_ref[b * NB:(b + 1) * NB, a * NB:(a + 1) * NB]
-                x = (x + y.T) * 0.5
+                x = (x + block(b, a).T) * 0.5
             s[a * NB:(a + 1) * NB, b * NB:(b + 1) * NB] = x
         if a + 1 < nb:
             s[a * NB:(a + 1) * NB, (a + 1) * NB:] = jnp.zeros((NB, n - (a + 1) * NB), jnp.float32)
     row0 = lax.axis_index("row") * TILE + lax.axis_index("col") * 8
     s[n:n + 8, :] = s[pl.ds(pl.multiple_of(row0, 8), 8), :]
     for t in range(1, m // 8):
-        s[n + 8 * t:n + 8 * t + 8, :] = jnp.where(where_ref[t:t + 1, :1] > 0.0, own_ref[8 * t:8 * t + 8, :], 0.0)
+        s[n + 8 * t:n + 8 * t + 8, :] = jnp.where(keep_ref[t:t + 1, :1] > 0.0, own_ref[8 * t:8 * t + 8, :], 0.0)
     return row0
 
 
@@ -214,33 +215,82 @@
     return [pltpu.SemaphoreType.DMA((2, 4, 4)) for _ in range(4)]
 
 
-def panel_body(message_ref, own_ref, diag_ref, label_ref, got_ref, share, front, units, packed, msg_send, msg_recv, local_sem,
-               f_send, f_recv, u_send, u_recv, send, recv, core_send, core_recv):
+MOVES = [(0, 0, 0), (0, 0, 1)]
+for group in (
+    ((1, 1), (3, 3)),
+    ((1, 3), (3, 1)),
+    ((1, 0), (3, 0), (0, 1), (0, 3)),
+    ((2, 0), (0, 2)),
+    ((2, 2),),
+    ((2, 1), (2, 3), (1, 2), (3, 2)),
+):
+    for dk in range(2):
+        MOVES += [(dy, dz, dk) for dy, dz in group]
+STARTS = {-2: (1, 6), -1: (6, 10), 1: (10, 14), 3: (14, 18), 5: (18, 22)}
+EARLY = (22, 24)
+LATER = (24, 32)
+
+
+def main_body(slot_ref, keep_ref, mark_ref, mirror_ref, front_ref, tiles_ref, out_ref, s, parts, own, labels, message, got, payload,
+              share, passed, units, g, across, arrived, high, low, m_send, m_recv, f_send, f_recv, u_send, u_recv,
+              a_send, a_recv, local_sem, x_send, x_recv, send, recv, core_send, core_recv,
+              d_send, d_recv, dcore_send, dcore_recv):
     r, c, y, z, k = here()
-    n_col = got_ref.shape[0]
-    slab = got_ref.shape[1]
-    lead = share.shape[1]
-    half = units.shape[3]
-    greet([(r, lax.rem(c + d, n_col)) for d in range(1, n_col)] + row_peers(r, c))
-
-    def message(d):
-        to = lax.rem(c + d, n_col)
+    n_col = arrived.shape[0]
+    lead = front_ref.shape[0]
+    slab = TILE // n_col
+    n = s.shape[1]
+    peers = [(r, lax.rem(c + d, n_col)) for d in range(1, n_col)] + row_peers(r, c)
+    barrier = pltpu.get_barrier_semaphore()
+    for device in peers:
+        pl.semaphore_signal(barrier, inc=1, device_id=device, device_id_type=MESH)
+    for q in range(4):
+        message[:, :, q * TILE:(q + 1) * TILE] = tiles_ref[slot_ref[q]].reshape(n_col, slab, TILE)
+    message[:, :, 4 * TILE:5 * TILE] = mirror_ref[...]
+    message[:, :, 5 * TILE:] = mark_ref[...]
+    got[c] = message[c]
+    pl.semaphore_wait(barrier, len(peers))
+
+    def letter(d):
+        dy, dz, dk = MOVES[d]
+        to = at_col(turn(y, dy), turn(z, dz), lax.rem(k + dk, 2))
         return pltpu.make_async_remote_copy(
-            src_ref=message_ref.at[to],
-            dst_ref=got_ref.at[c],
-            send_sem=msg_send.at[d],
-            recv_sem=msg_recv.at[d],
+            src_ref=message.at[to], dst_ref=got.at[c], send_sem=m_send.at[d], recv_sem=m_recv.at[d], device_id=(r, to),
+            device_id_type=MESH,
+        )
+
+    letters = [letter(d) for d in range(1, n_col)]
+    for copy in letters:
+        copy.start()
+    for q in range(n_col):
+        payload[q] = tiles_ref[slot_ref[q]]
+
+    def tile(d):
+        dy, dz, dk = MOVES[d]
+        to = at_col(turn(y, dy), turn(z, dz), lax.rem(k + dk, 2))
+        return to, pltpu.make_async_remote_copy(
+            src_ref=payload.at[to],
+            dst_ref=arrived.at[d],
+            send_sem=a_send.at[d],
+            recv_sem=a_recv.at[d],
             device_id=(r, to),
             device_id_type=MESH,
         )
 
-    keep = pltpu.make_async_copy(message_ref.at[c], got_ref.at[c], local_sem.at[0])
-    keep.start()
-    for d in range(1, n_col):
-        message(d).start()
-    keep.wait()
-    for d in range(1, n_col):
-        message(d).wait_recv()
+    def begin(ds):
+        for d in range(*ds):
+            to, copy = tile(d)
+
+            @pl.when(to >= 4)
+            def _(copy=copy):
+                copy.start()
+
+    begin(STARTS[-2])
+    arrived[0] = payload[c]
+    for t in range(lead):
+        out_ref[t] = front_ref[t]
+    for copy in letters:
+        copy.wait_recv()
 
     def exchange(src, dst, s_sem, r_sem, d):
         return pltpu.make_async_remote_copy(
@@ -250,133 +300,56 @@
 
     for q in range(4):
         for t in range(lead):
-            share[q, t] = got_ref[4 * t + q, :, 4 * TILE:5 * TILE]
-    front[r] = share[r]
-    shares = [exchange(share.at[turn(r, d)], front.at[r], f_send, f_recv, d) for d in range(1, 4)]
+            share[q, t] = got[4 * t + q, :, 4 * TILE:5 * TILE]
+    passed[r] = share[r]
+    shares = [exchange(share.at[turn(r, d)], passed.at[r], f_send, f_recv, d) for d in range(1, 4)]
     for copy in shares:
         copy.start()
-    label_ref[...] = got_ref[:, 4, 5 * TILE:5 * TILE + 128]
-    own_ref[...] = jnp.zeros_like(own_ref)
-
-    def add(s, carry):
+    labels[...] = got[:, 4, 5 * TILE:5 * TILE + 128]
+    own[...] = jnp.zeros_like(own)
+
+    def add(i, carry):
         for q in range(4):
             at = slice(q * TILE, (q + 1) * TILE)
-            label = got_ref[s, q:q + 1, 5 * TILE:5 * TILE + 128]
-            label = jnp.broadcast_to(jnp.concatenate([label, label], axis=1), (slab, TILE))
-            part = got_ref[s, :, at]
+            acc = [own[t * slab:(t + 1) * slab, at] for t in range(lead)]
+            for e in range(8):
+                label = got[i * 8 + e, q:q + 1, 5 * TILE:5 * TILE + 128]
+                label = jnp.broadcast_to(jnp.concatenate([label, label], axis=1), (slab, TILE))
+                part_in = got[i * 8 + e, :, at]
+                for t in range(lead):
+                    acc[t] = acc[t] + jnp.where(label == float(t), part_in, 0.0)
             for t in range(lead):
-                rows = slice(t * slab, (t + 1) * slab)
-                own_ref[rows, at] = own_ref[rows, at] + jnp.where(label == float(t), part, 0.0)
+                own[t * slab:(t + 1) * slab, at] = acc[t]
         return carry
 
-    lax.fori_loop(0, n_col, add, 0)
+    lax.fori_loop(0, n_col // 8, add, 0)
     for copy in shares:
         copy.wait_recv()
     for q in range(4):
         at = slice(q * TILE, (q + 1) * TILE)
         for t in range(lead):
             rows = slice(t * slab, (t + 1) * slab)
-            own_ref[rows, at] = own_ref[rows, at] + front[q, t]
+            own[rows, at] = own[rows, at] + passed[q, t]
     for p in range(2):
-        units[r, p] = own_ref[:slab, p * half:(p + 1) * half]
+        units[r, p] = own[:slab, p * n // 2:(p + 1) * n // 2]
     lines = [exchange(units.at[r], units.at[r], u_send, u_recv, d) for d in range(1, 4)]
     for copy in lines:
         copy.start()
     for copy in lines:
         copy.wait_recv()
-    for q in range(4):
-        packed[q] = units[q, 0]
-    for q in range(2):
-        packed[4 + q] = units[2 + q, 1]
-    diag_ref[y, z, k] = packed[...]
-
-    def piece(h, yy, zz, kk):
-        return diag_ref.at[yy, zz, kk, pl.ds(h * 3, 3)]
-
-    finish = plane_gather(piece, send, recv, core_send, core_recv, r, y, z, k)
-    for d in range(1, n_col):
-        message(d).wait_send()
-    for copy in shares + lines:
-        copy.wait_send()
-    finish()
-
-
-def panel_call(message, lead):
-    n_col, slab, width = message.shape
-    half = 2 * TILE
-    dma = pltpu.SemaphoreType.DMA
-    vmem = pl.BlockSpec(memory_space=pltpu.VMEM)
-    return pl.pallas_call(
-        panel_body,
-        out_shape=[
-            jax.ShapeDtypeStruct((lead * slab, 4 * TILE), jnp.float32),
-            jax.ShapeDtypeStruct((4, 4, 2, 6, slab, half), jnp.float32),
-            jax.ShapeDtypeStruct((n_col, 128), jnp.float32),
-        ],
-        in_specs=[vmem],
-        out_specs=[vmem] * 3,
-        scratch_shapes=[
-            pltpu.VMEM((n_col, slab, width), jnp.float32),
-            pltpu.VMEM((4, lead, slab, TILE), jnp.float32),
-            pltpu.VMEM((4, lead, slab, TILE), jnp.float32),
-            pltpu.VMEM((4, 2, slab, half), jnp.float32),
-            pltpu.VMEM((6, slab, half), jnp.float32),
-            dma((n_col,)),
-            dma((n_col,)),
-            dma((1,)),
-            dma((4,)),
-            dma((4,)),
-            dma((4,)),
-            dma((4,)),
-        ]
-        + gather_sems(),
-        compiler_params=pltpu.CompilerParams(collective_id=0, has_side_effects=True, vmem_limit_bytes=56 * MIB),
-        cost_estimate=pl.CostEstimate(flops=0, bytes_accessed=1000, transcendentals=0),
-    )(message)
-
-
-def main_body(keep_ref, label_ref, parts_ref, own_ref, front_ref, payload_ref, out_ref, s, diag, g, across, arrived, high, low,
-              a_send, a_recv, local_sem, x_send, x_recv, send, recv, core_send, core_recv):
-    r, c, y, z, k = here()
-    n_col = arrived.shape[0]
-    lead = front_ref.shape[0]
-    n = s.shape[1]
-    greet([(r, lax.rem(c + d, n_col)) for d in range(1, n_col)] + row_peers(r, c))
-
-    def tile(d):
-        to = lax.rem(c + d, n_col)
-        return pltpu.make_async_remote_copy(
-            src_ref=payload_ref.at[to],
-            dst_ref=arrived.at[d],
-            send_sem=a_send.at[d],
-            recv_sem=a_recv.at[d],
-            device_id=(r, to),
-            device_id_type=MESH,
-        )
-
-    def begin(ds):
-        for d in ds:
-            @pl.when(lax.rem(c + d, n_col) >= 4)
-            def _(d=d):
-                tile(d).start()
-
-    own_tile = pltpu.make_async_copy(payload_ref.at[c], arrived.at[0], local_sem.at[0])
-    own_tile.start()
-    order = list(range(1, n_col))
-    plan = [3, 2, 2, 2, 2, 2, 2, 1]
-    groups = []
-    for size in plan:
-        groups.append(order[:size])
-        order = order[size:]
-    row0 = None
-    begin(groups[0])
-    row0 = load_diag(parts_ref, own_ref, keep_ref, diag, s)
-    for t in range(lead):
-        out_ref[t] = front_ref[t]
+    parts[y, z, k] = jnp.concatenate([units[:, 0], units[2:, 1]], axis=0)
+
+    def unit(h, yy, zz, kk):
+        return parts.at[yy, zz, kk, pl.ds(h * 3, 3)]
+
+    close = plane_gather(unit, d_send, d_recv, dcore_send, dcore_recv, r, y, z, k)
+    begin(STARTS[-1])
+    close()
+    row0 = load_diag(parts, own, keep_ref, s)
     for step in range(n // NB):
-        if step:
-            begin(groups[step])
         factor_step(s, step)
+        if step in STARTS:
+            begin(STARTS[step])
     m = s.shape[0] - n
     ids = lax.broadcasted_iota(jnp.int32, (m, n), 0)
     lane = lax.broadcasted_iota(jnp.int32, (m, n), 1)
@@ -412,23 +385,23 @@
                 for d in range(1, 4):
                     cross(h, da, mate, d).start()
 
-    later = order
-
     def early():
-        begin(later[:4])
+        begin(EARLY)
 
     finish = plane_gather(piece, send, recv, core_send, core_recv, r, y, z, k, early, forward)
-    begin(later[4:])
+    begin(LATER)
 
     def absorb(ds):
         @pl.when(c >= 4)
         def _():
             for d in ds:
                 if d:
-                    tile(d).wait_recv()
-            wanted = [
-                jnp.concatenate([label_ref[pl.ds(lax.rem(c + n_col - d, n_col), 1), :]] * 2, axis=1) for d in ds
-            ]
+                    tile(d)[1].wait_recv()
+            wanted = []
+            for d in ds:
+                dy, dz, dk = MOVES[d]
+                origin = at_col(turn(y, 4 - dy), turn(z, 4 - dz), lax.rem(k + dk, 2))
+                wanted.append(jnp.concatenate([labels[pl.ds(origin, 1), :]] * 2, axis=1))
 
             def strip(i, carry):
                 rows = pl.ds(pl.multiple_of(i * 8, 8), 8)
@@ -444,8 +417,8 @@
 
             lax.fori_loop(0, TILE // 8, strip, 0)
 
-    own_tile.wait()
-    absorb([0] + sum(groups[:4], []))
+    absorb(range(0, 10))
+    absorb(range(10, 18))
     finish()
 
     @pl.when(r == source)
@@ -478,21 +451,19 @@
 
         lax.fori_loop(1, lead, update, 0)
 
-    absorb(sum(groups[4:], []))
-    rest = list(later)
-    while rest:
-        size = 4 if len(rest) > 6 else 2
-        absorb(rest[:size])
-        rest = rest[size:]
+    for lo, hi in ((18, 24), (24, 28), (28, 32)):
+        absorb(range(lo, hi))
 
     @pl.when(c >= 4)
     def _():
         out_ref[0] = jnp.zeros((TILE, TILE), jnp.float32)
 
     for d in range(1, n_col):
-        @pl.when(lax.rem(c + d, n_col) >= 4)
-        def _(d=d):
-            tile(d).wait_send()
+        to, copy = tile(d)
+
+        @pl.when(to >= 4)
+        def _(copy=copy):
+            copy.wait_send()
 
     for h in range(2):
         @pl.when((r == source) & (part == h))
@@ -501,57 +472,55 @@
                 for da in range(4):
                     for d in range(1, 4):
                         cross(h, da, mate, d).wait_send()
-
-
-def main_call(keep, labels, parts, own, blocks, payload):
+    for copy in letters + shares + lines:
+        copy.wait_send()
+
+
+def main_call(slots, keep, marks, mirrored, blocks, tiles):
     lead = blocks.shape[0]
-    n_col = payload.shape[0]
-    m, n = own.shape
+    n_col, slab, _ = mirrored.shape
+    n = 4 * TILE
     dma = pltpu.SemaphoreType.DMA
+    f32 = jnp.float32
     vmem = pl.BlockSpec(memory_space=pltpu.VMEM)
     return pl.pallas_call(
         main_body,
-        out_shape=jax.ShapeDtypeStruct(blocks.shape, jnp.float32),
-        in_specs=[vmem] * 5 + [pl.BlockSpec(memory_space=pl.ANY)],
+        out_shape=jax.ShapeDtypeStruct(blocks.shape, f32),
+        in_specs=[pl.BlockSpec(memory_space=pltpu.SMEM)] + [vmem] * 5,
         out_specs=vmem,
         scratch_shapes=[
-            pltpu.VMEM((n + m, n), jnp.float32),
-            pltpu.VMEM((n, n), jnp.float32),
-            pltpu.VMEM((4, 4, 2, lead, m // lead, n), jnp.float32),
-            pltpu.VMEM((4, 4, 2, m // lead, n), jnp.float32),
-            pltpu.VMEM((n_col, TILE, TILE), jnp.float32),
+            pltpu.VMEM((n + lead * slab, n), f32),
+            pltpu.VMEM((4, 4, 2, 6, slab, n // 2), f32),
+            pltpu.VMEM((lead * slab, n), f32),
+            pltpu.VMEM((n_col, 128), f32),
+            pltpu.VMEM((n_col, slab, 5 * TILE + 128), f32),
+            pltpu.VMEM((n_col, slab, 5 * TILE + 128), f32),
+            pltpu.VMEM(tiles.shape, f32),
+            pltpu.VMEM((4, lead, slab, TILE), f32),
+            pltpu.VMEM((4, lead, slab, TILE), f32),
+            pltpu.VMEM((4, 2, slab, n // 2), f32),
+            pltpu.VMEM((4, 4, 2, lead, slab, n), f32),
+            pltpu.VMEM((4, 4, 2, slab, n), f32),
+            pltpu.VMEM((n_col, TILE, TILE), f32),
             pltpu.VMEM((TILE, n), jnp.bfloat16),
             pltpu.VMEM((TILE, n), jnp.bfloat16),
+            dma((n_col,)),
+            dma((n_col,)),
+            dma((4,)),
+            dma((4,)),
+            dma((4,)),
+            dma((4,)),
             dma((n_col,)),
             dma((n_col,)),
             dma((2,)),
             dma((2, 4, 4)),
             dma((2, 4)),
         ]
+        + gather_sems()
         + gather_sems(),
-        compiler_params=pltpu.CompilerParams(collective_id=1, has_side_effects=True, vmem_limit_bytes=58 * MIB),
+        compiler_params=pltpu.CompilerParams(collective_id=0, has_side_effects=True, vmem_limit_bytes=60 * MIB),
         cost_estimate=pl.CostEstimate(flops=0, bytes_accessed=1000, transcendentals=0),
-    )(keep, labels, parts, own, blocks, payload)
-
-
-def pack_body(slot_ref, tile_ref, out_ref):
-    out_ref[...] = tile_ref[...]
-
-
-def pack_call(slots, tiles):
-    n = slots.shape[0]
-    t = tiles.shape[1]
-    return pl.pallas_call(
-        pack_body,
-        out_shape=jax.ShapeDtypeStruct((n, t, t), tiles.dtype),
-        grid_spec=pltpu.PrefetchScalarGridSpec(
-            num_scalar_prefetch=1,
-            grid=(n,),
-            in_specs=[pl.BlockSpec((1, t, t), lambda q, slot: (slot[q], 0, 0))],
-            out_specs=pl.BlockSpec((1, t, t), lambda q, slot: (q, 0, 0)),
-        ),
-        cost_estimate=pl.CostEstimate(flops=0, bytes_accessed=n * t * t * 8, transcendentals=0),
-    )(slots, tiles)
+    )(slots, keep, marks, mirrored, blocks, tiles)
 
 
 def local(front, child_tiles, child_owner, child_place, child_count, tile_mask):
@@ -573,20 +542,15 @@
     label = jnp.sum(jnp.where(hit & (ids < count)[None, :], place[None, :] + 1, 0), axis=1) - 1
     label_f = label.astype(jnp.float32)
 
-    panel_tiles = pack_call(slot_of[:4], tiles)
-    slabs = panel_tiles.reshape(4, n_col, slab, TILE).transpose(1, 2, 0, 3).reshape(n_col, slab, 4 * TILE)
     mirrored = blocks[0].T.reshape(n_col, slab, TILE)
     marks = jnp.concatenate(
         [jnp.broadcast_to(label_f[None, :4], (n_col, 4)), label_f[:, None], jnp.zeros((n_col, slab - 5), jnp.float32)], axis=1
     )
     marks = jnp.broadcast_to(marks[:, :, None], (n_col, slab, 128))
-    message = jnp.concatenate([slabs, mirrored, marks], axis=2)
-    own, parts, labels = panel_call(message, lead)
-    payload = pack_call(slot_of, tiles)
     row_tiles = jnp.arange(lead, dtype=jnp.int32) * n_row + row_id
     keep = jnp.sum(jnp.where(row_tiles[:, None] == jnp.arange(tile_mask.shape[0])[None, :], tile_mask[None, :], 0), axis=1)
     keep = jnp.broadcast_to(keep.astype(jnp.float32)[:, None], (lead, 128))
-    result = main_call(keep, labels, parts, own, blocks, payload)
+    result = main_call(slot_of, keep, marks, mirrored, blocks, tiles)
     return result.reshape(front.shape)
 
 

time: 301 us -> 210 us (0.70)
  the two profiles are of different devices: /device:TPU:113 before, /device:TPU:48 now
where the time goes in v4:
time: 210 us; the launch traced here: 208 us
  Pallas kernels  192 us (91%)
  local copies, waits for them, and re-layouts  11.7 us (6%)
  other arithmetic  2.96 us (1%)
    pallas_call x1, Pallas kernels, main_call(): pl.pallas_call(main_body, out_shape=jax.ShapeDtypeStruct(blocks.shape, f3...  192 us
    reshape x1, local copies, waits for them, and re-layouts, local(): return result.reshape(front.shape)  5.08 us

profile of v4, /device:TPU:48, one launch (start us, length us, event | category | flops | bytes accessed | tf_op | source)
XLA Modules:
  0.0 207.6 jit_solution(17318174912197651628)
XLA Ops:
  0.7 0.8 select_reduce_fusion.2
  1.5 0.7 add_bitcast_fusion
  2.2 1.4 select_reduce_fusion
  3.6 0.1 pad.2.clone
  3.6 0.1 maximum_maximum_fusion
  3.7 0.7 broadcast_in_dim.62.keep_ref
  4.4 0.1 copy.13
  4.5 0.7 broadcast_in_dim.66.mark_ref
  5.2 1.1 slice.8
  6.3 0.9 copy.18
  7.2 3.0 %copy.20 = f32[8,1,256,1,1,256]{5,2,3,4,1,0:T(8,128)} copy(f32[8,1,256,1,1,256]{5,4,3,2,1,0:T(1,128)} %param.6) | data formatting | bytes 4194304
  10.2 192.2 %shard_map.64 = f32[8,256,256]{2,1,0:T(8,128)} custom-call(s32[32]{0:T(128)} %get-tuple-element.6.slot_ref, f32[8,128]{1,0:T(8,128)} %broadcast_in_dim.62.keep_ref, f32[32,8,128]{2,1,0:T(8,128)} %broadcast_in_dim.66.mark_ref, f32[32,8,256]{2,1,0:T(8,128)} %bitcast.22, f32[8,256,256]{2,1,0:T(8,128)} %bitcast.21, f32[32,256,256]{2,1,0:T(8,128)} %bitcast.19), custom_call_target="tpu_custom_call" | custom-call | bytes 1000 | tf_op jit(solution)/shard_map/pallas_call | solution.py:486
  202.5 5.1 %copy.15 = f32[8,1,256,1,1,256]{5,4,3,2,1,0:T(1,128)} copy(f32[8,1,256,1,1,256]{5,2,0,4,3,1:T(8,128)} %bitcast.20) | data formatting | bytes 4194304 | tf_op jit(solution)/shard_map/reshape | solution.py:554
  (6 shorter events, 0.0 us)

commit v5 on v4

--- a/solution.py
+++ b/solution.py
@@ -56,17 +56,20 @@
             rest = rest[SB:] - dot_tn(r[:, lo:NB], r)
     return jnp.concatenate(done, axis=0)
 
-def load_diag(part_ref, own_ref, keep_ref, s):
+def load_diag(left, right, lower, own_ref, mask_ref, s):
     n = s.shape[1]
     m = own_ref.shape[0]
     nb = n // NB
     half = nb // 2
 
     def block(a, b):
-        unit = a // 2 + (2 if b >= half else 0)
-        at = b % half * NB
         y = a % 2 * 2
-        return part_ref[y:y + 2, :, :, unit, :, at:at + NB].reshape(NB, NB)
+        if b >= half:
+            ref, q = lower, a // 2 - 2
+        else:
+            ref, q = (left, right)[b // 2], a // 2
+        at = (b % half if b >= half else b % 2) * NB
+        return ref[q, y:y + 2, :, :, :, at:at + NB].reshape(NB, NB)
 
     for a in range(nb):
         for b in range(a + 1):
@@ -76,10 +79,11 @@
             s[a * NB:(a + 1) * NB, b * NB:(b + 1) * NB] = x
         if a + 1 < nb:
             s[a * NB:(a + 1) * NB, (a + 1) * NB:] = jnp.zeros((NB, n - (a + 1) * NB), jnp.float32)
-    row0 = lax.axis_index("row") * TILE + lax.axis_index("col") * 8
+    r = lax.axis_index("row")
+    row0 = r * TILE + lax.axis_index("col") * 8
     s[n:n + 8, :] = s[pl.ds(pl.multiple_of(row0, 8), 8), :]
     for t in range(1, m // 8):
-        s[n + 8 * t:n + 8 * t + 8, :] = jnp.where(keep_ref[t:t + 1, :1] > 0.0, own_ref[8 * t:8 * t + 8, :], 0.0)
+        s[n + 8 * t:n + 8 * t + 8, :] = jnp.where(mask_ref[4 * t + r] == 1, own_ref[8 * t:8 * t + 8, :], 0.0)
     return row0
 
 
@@ -231,23 +235,134 @@
 LATER = (24, 32)
 
 
-def main_body(slot_ref, keep_ref, mark_ref, mirror_ref, front_ref, tiles_ref, out_ref, s, parts, own, labels, message, got, payload,
-              share, passed, units, g, across, arrived, high, low, m_send, m_recv, f_send, f_recv, u_send, u_recv,
+def cube_gather(left, right, lower, send, recv, core_send, core_recv, r, y, z, k):
+    me = {"x": r, "y": y, "z": z}
+    refs = (left, right, lower)
+    axes = (("y", "z", "x"), ("z", "x", "y"), ("x", "y", "z"))
+
+    def peer(axis, d):
+        at = dict(me)
+        at[axis] = turn(at[axis], d)
+        return (at["x"], at_col(at["y"], at["z"], k))
+
+    def view(part, last, e):
+        at = {}
+        for i, axis in enumerate(axes[part]):
+            at[axis] = slice(None) if i < last else turn(me[axis], 4 - e) if i == last else me[axis]
+        if part == 2:
+            at["x"] = slice(None)
+        return refs[part].at[at["x"], at["y"], at["z"], k]
+
+    sent = []
+
+    def push(ref, to, s_sem, r_sem):
+        copy = pltpu.make_async_remote_copy(
+            src_ref=ref, dst_ref=ref, send_sem=s_sem, recv_sem=r_sem, device_id=to, device_id_type=MESH
+        )
+        copy.start()
+        sent.append(copy)
+        return copy
+
+    arrive = {}
+
+    def phase(part, p, e):
+        ref = view(part, p - 1, e) if p else view(part, 0, 0)
+        for d in range(1, 4):
+            arrive[part, p, e, d] = push(ref, peer(axes[part][p], d), send.at[part, p, e, d], recv.at[part, p, e, d])
+
+    core = []
+
+    def mate(part, e):
+        core.append(push(view(part, 2, e), (r, at_col(y, z, 1 - k)), core_send.at[part, e], core_recv.at[part, e]))
+
+    def corner(d):
+        ref = lower.at[r - 2, y, z, k]
+        return pltpu.make_async_remote_copy(
+            src_ref=ref, dst_ref=ref, send_sem=send.at[2, 0, 0, d], recv_sem=recv.at[2, 0, 0, d], device_id=peer("x", d),
+            device_id_type=MESH,
+        )
+
+    @pl.when(r >= 2)
+    def _():
+        for d in range(1, 4):
+            corner(d).start()
+
+    for part in range(2):
+        phase(part, 0, 0)
+    for part in range(2):
+        phase(part, 1, 0)
+    for e in range(1, 4):
+        for part in range(2):
+            arrive[part, 0, 0, e].wait_recv()
+            phase(part, 1, e)
+    for d in range(1, 4):
+        @pl.when(turn(r, 4 - d) >= 2)
+        def _(d=d):
+            ref = lower.at[0, y, z, k]
+            pltpu.make_async_remote_copy(
+                src_ref=ref, dst_ref=ref, send_sem=send.at[2, 0, 0, d], recv_sem=recv.at[2, 0, 0, d], device_id=peer("x", d),
+                device_id_type=MESH,
+            ).wait_recv()
+    phase(2, 1, 0)
+    for part in (2, 0, 1):
+        phase(part, 2, 0)
+    for e in range(1, 4):
+        for part in range(2):
+            for f in range(4):
+                arrive[part, 1, f, e].wait_recv()
+            phase(part, 2, e)
+        arrive[2, 1, 0, e].wait_recv()
+        phase(2, 2, e)
+    for part in range(3):
+        mate(part, 0)
+    for e in range(1, 4):
+        for part in range(3):
+            for f in range(4):
+                arrive[part, 2, f, e].wait_recv()
+            mate(part, e)
+
+    def finish():
+        for copy in core:
+            copy.wait_recv()
+        for copy in sent:
+            copy.wait_send()
+
+        @pl.when(r >= 2)
+        def _():
+            for d in range(1, 4):
+                corner(d).wait_send()
+
+    return finish
+
+
+def main_body(slot_ref, mark_ref, mask_ref, front_ref, child_ref, out_ref, s, left, right, lower, own, labels, message, got, payload,
+              tiles_ref, held, share, passed, g, across, arrived, high, low, m_send, m_recv, f_send, f_recv,
               a_send, a_recv, local_sem, x_send, x_recv, send, recv, core_send, core_recv,
               d_send, d_recv, dcore_send, dcore_recv):
     r, c, y, z, k = here()
     n_col = arrived.shape[0]
-    lead = front_ref.shape[0]
+    lead = out_ref.shape[0]
     slab = TILE // n_col
     n = s.shape[1]
+    fetch = pltpu.make_async_copy(front_ref.at[:, 0], held, local_sem.at[0])
+    fetch.start()
+    fill = pltpu.make_async_copy(child_ref, tiles_ref, local_sem.at[2])
+    fill.start()
     peers = [(r, lax.rem(c + d, n_col)) for d in range(1, n_col)] + row_peers(r, c)
     barrier = pltpu.get_barrier_semaphore()
     for device in peers:
         pl.semaphore_signal(barrier, inc=1, device_id=device, device_id_type=MESH)
+    sub = lax.broadcasted_iota(jnp.int32, (slab, 128), 0)
+    base = jnp.zeros((slab, 128), jnp.float32)
+    for q in range(4):
+        base = jnp.where(sub == q, mark_ref[q], base)
+    for q in range(n_col):
+        message[q, :, 5 * TILE:] = jnp.where(sub == 4, mark_ref[q], base)
+    fetch.wait()
+    message[:, :, 4 * TILE:5 * TILE] = held[:TILE].T.reshape(n_col, slab, TILE)
+    fill.wait()
     for q in range(4):
         message[:, :, q * TILE:(q + 1) * TILE] = tiles_ref[slot_ref[q]].reshape(n_col, slab, TILE)
-    message[:, :, 4 * TILE:5 * TILE] = mirror_ref[...]
-    message[:, :, 5 * TILE:] = mark_ref[...]
     got[c] = message[c]
     pl.semaphore_wait(barrier, len(peers))
 
@@ -288,7 +403,7 @@
     begin(STARTS[-2])
     arrived[0] = payload[c]
     for t in range(lead):
-        out_ref[t] = front_ref[t]
+        out_ref[t] = held[t * TILE:(t + 1) * TILE]
     for copy in letters:
         copy.wait_recv()
 
@@ -330,22 +445,17 @@
         for t in range(lead):
             rows = slice(t * slab, (t + 1) * slab)
             own[rows, at] = own[rows, at] + passed[q, t]
-    for p in range(2):
-        units[r, p] = own[:slab, p * n // 2:(p + 1) * n // 2]
-    lines = [exchange(units.at[r], units.at[r], u_send, u_recv, d) for d in range(1, 4)]
-    for copy in lines:
-        copy.start()
-    for copy in lines:
-        copy.wait_recv()
-    parts[y, z, k] = jnp.concatenate([units[:, 0], units[2:, 1]], axis=0)
-
-    def unit(h, yy, zz, kk):
-        return parts.at[yy, zz, kk, pl.ds(h * 3, 3)]
-
-    close = plane_gather(unit, d_send, d_recv, dcore_send, dcore_recv, r, y, z, k)
+    left[r, y, z, k] = own[:slab, :TILE]
+    right[r, y, z, k] = own[:slab, TILE:2 * TILE]
+
+    @pl.when(r >= 2)
+    def _():
+        lower[r - 2, y, z, k] = own[:slab, 2 * TILE:]
+
+    close = cube_gather(left, right, lower, d_send, d_recv, dcore_send, dcore_recv, r, y, z, k)
     begin(STARTS[-1])
     close()
-    row0 = load_diag(parts, own, keep_ref, s)
+    row0 = load_diag(left, right, lower, own, mask_ref, s)
     for step in range(n // NB):
         factor_step(s, step)
         if step in STARTS:
@@ -472,33 +582,37 @@
                 for da in range(4):
                     for d in range(1, 4):
                         cross(h, da, mate, d).wait_send()
-    for copy in letters + shares + lines:
+    for copy in letters + shares:
         copy.wait_send()
 
 
-def main_call(slots, keep, marks, mirrored, blocks, tiles):
-    lead = blocks.shape[0]
-    n_col, slab, _ = mirrored.shape
+def main_call(slots, marks, mask, front, tiles):
+    n_col = tiles.shape[0]
+    slab = TILE // n_col
     n = 4 * TILE
+    lead = front.shape[0] // TILE
     dma = pltpu.SemaphoreType.DMA
     f32 = jnp.float32
-    vmem = pl.BlockSpec(memory_space=pltpu.VMEM)
+    smem = pl.BlockSpec(memory_space=pltpu.SMEM)
     return pl.pallas_call(
         main_body,
-        out_shape=jax.ShapeDtypeStruct(blocks.shape, f32),
-        in_specs=[pl.BlockSpec(memory_space=pltpu.SMEM)] + [vmem] * 5,
-        out_specs=vmem,
+        out_shape=jax.ShapeDtypeStruct((lead, TILE, TILE), f32),
+        in_specs=[smem] * 3 + [pl.BlockSpec(memory_space=pl.ANY)] * 2,
+        out_specs=pl.BlockSpec(memory_space=pltpu.VMEM),
         scratch_shapes=[
             pltpu.VMEM((n + lead * slab, n), f32),
-            pltpu.VMEM((4, 4, 2, 6, slab, n // 2), f32),
+            pltpu.VMEM((4, 4, 4, 2, slab, TILE), f32),
+            pltpu.VMEM((4, 4, 4, 2, slab, TILE), f32),
+            pltpu.VMEM((2, 4, 4, 2, slab, 2 * TILE), f32),
             pltpu.VMEM((lead * slab, n), f32),
             pltpu.VMEM((n_col, 128), f32),
             pltpu.VMEM((n_col, slab, 5 * TILE + 128), f32),
             pltpu.VMEM((n_col, slab, 5 * TILE + 128), f32),
             pltpu.VMEM(tiles.shape, f32),
+            pltpu.VMEM(tiles.shape, f32),
+            pltpu.VMEM((lead * TILE, TILE), f32),
             pltpu.VMEM((4, lead, slab, TILE), f32),
             pltpu.VMEM((4, lead, slab, TILE), f32),
-            pltpu.VMEM((4, 2, slab, n // 2), f32),
             pltpu.VMEM((4, 4, 2, lead, slab, n), f32),
             pltpu.VMEM((4, 4, 2, slab, n), f32),
             pltpu.VMEM((n_col, TILE, TILE), f32),
@@ -508,49 +622,31 @@
             dma((n_col,)),
             dma((4,)),
             dma((4,)),
-            dma((4,)),
-            dma((4,)),
             dma((n_col,)),
             dma((n_col,)),
-            dma((2,)),
+            dma((3,)),
             dma((2, 4, 4)),
             dma((2, 4)),
         ]
         + gather_sems()
-        + gather_sems(),
+        + [dma((3, 3, 4, 4)), dma((3, 3, 4, 4)), dma((3, 4)), dma((3, 4))],
         compiler_params=pltpu.CompilerParams(collective_id=0, has_side_effects=True, vmem_limit_bytes=60 * MIB),
         cost_estimate=pl.CostEstimate(flops=0, bytes_accessed=1000, transcendentals=0),
-    )(slots, keep, marks, mirrored, blocks, tiles)
+    )(slots, marks, mask, front, tiles)
 
 
 def local(front, child_tiles, child_owner, child_place, child_count, tile_mask):
-    n_row = lax.axis_size("row")
     n_col = lax.axis_size("col")
-    row_id = lax.axis_index("row")
-    col_id = lax.axis_index("col")
     lead = front.shape[0]
-    slab = TILE // n_col
     slots = child_tiles.shape[2]
-    blocks = front.reshape(lead, TILE, TILE)
-    tiles = child_tiles.reshape(slots, TILE, TILE)
     owner = child_owner.reshape(slots)
     place = child_place.reshape(slots)
     count = child_count.reshape(())
     ids = jnp.arange(slots, dtype=jnp.int32)
     hit = owner[None, :] == jnp.arange(n_col, dtype=jnp.int32)[:, None]
     slot_of = jnp.sum(jnp.where(hit, ids[None, :], 0), axis=1)
-    label = jnp.sum(jnp.where(hit & (ids < count)[None, :], place[None, :] + 1, 0), axis=1) - 1
-    label_f = label.astype(jnp.float32)
-
-    mirrored = blocks[0].T.reshape(n_col, slab, TILE)
-    marks = jnp.concatenate(
-        [jnp.broadcast_to(label_f[None, :4], (n_col, 4)), label_f[:, None], jnp.zeros((n_col, slab - 5), jnp.float32)], axis=1
-    )
-    marks = jnp.broadcast_to(marks[:, :, None], (n_col, slab, 128))
-    row_tiles = jnp.arange(lead, dtype=jnp.int32) * n_row + row_id
-    keep = jnp.sum(jnp.where(row_tiles[:, None] == jnp.arange(tile_mask.shape[0])[None, :], tile_mask[None, :], 0), axis=1)
-    keep = jnp.broadcast_to(keep.astype(jnp.float32)[:, None], (lead, 128))
-    result = main_call(slot_of, keep, marks, mirrored, blocks, tiles)
+    marks = (jnp.sum(jnp.where(hit & (ids < count)[None, :], place[None, :] + 1, 0), axis=1) - 1).astype(jnp.float32)
+    result = main_call(slot_of, marks, tile_mask, front.reshape(lead * TILE, 1, TILE), child_tiles.reshape(slots, TILE, TILE))
     return result.reshape(front.shape)
 
 

time: 210 us -> 202 us (0.962)
  local copies, waits for them, and re-layouts: 11.7 us -> 5.08 us
    unnamed x1 -> x0, local copies, waits for them, and re-layouts: 3.04 us -> none
where the time goes in v5:
time: 202 us; the launch traced here: 199 us
  Pallas kernels  191 us (95%)
  local copies, waits for them, and re-layouts  5.08 us (3%)
  other arithmetic  2.47 us (1%)
    pallas_call x1, Pallas kernels, main_call(): pl.pallas_call(main_body, out_shape=jax.ShapeDtypeStruct((lead, TILE, TIL...  191 us
    reshape x1, local copies, waits for them, and re-layouts, local(): return result.reshape(front.shape)  5.08 us

profile of v5, /device:TPU:48, one launch (start us, length us, event | category | flops | bytes accessed | tf_op | source)
XLA Modules:
  0.0 198.8 jit_solution(7599409245474120282)
XLA Ops:
  0.7 0.7 add_bitcast_fusion
  1.3 1.3 select_reduce_fusion
  2.6 0.5 add_convert_fusion.mark_ref
  3.1 190.6 %shard_map.64 = f32[8,256,256]{2,1,0:T(8,128)} custom-call(s32[32]{0:T(128)} %get-tuple-element.6.slot_ref, f32[32]{0:T(128)} %add_convert_fusion.mark_ref, s32[32]{0:T(128)} %mask_ref.1, f32[2048,1,256]{2,1,0:T(1,128)} %bitcast.10, f32[32,256,256]{2,1,0:T(8,128)} %bitcast.9), custom_call_target="tpu_custom_call" | custom-call | bytes 1000 | tf_op jit(solution)/shard_map/pallas_call | solution.py:597
  193.7 5.1 %copy.8 = f32[8,1,256,1,1,256]{5,4,3,2,1,0:T(1,128)} copy(f32[8,1,256,1,1,256]{5,2,0,4,3,1:T(8,128)} %bitcast.8) | data formatting | bytes 4194304 | tf_op jit(solution)/shard_map/reshape | solution.py:650
  (1 shorter events, 0.0 us)

commit v6 on v5

--- a/solution.py
+++ b/solution.py
@@ -230,9 +230,9 @@
 ):
     for dk in range(2):
         MOVES += [(dy, dz, dk) for dy, dz in group]
-STARTS = {-2: (1, 6), -1: (6, 10), 1: (10, 14), 3: (14, 18), 5: (18, 22)}
-EARLY = (22, 24)
-LATER = (24, 32)
+STARTS = {-2: (1, 6), -1: (6, 14), 0: (14, 18), 2: (18, 22), 4: (22, 28)}
+EARLY = (28, 28)
+LATER = (28, 32)
 
 
 def cube_gather(left, right, lower, send, recv, core_send, core_recv, r, y, z, k):
@@ -335,13 +335,13 @@
     return finish
 
 
-def main_body(slot_ref, mark_ref, mask_ref, front_ref, child_ref, out_ref, s, left, right, lower, own, labels, message, got, payload,
+def main_body(slot_ref, mark_ref, mask_ref, front_ref, child_ref, out_ref, total, s, left, right, lower, own, labels, message, got, payload,
               tiles_ref, held, share, passed, g, across, arrived, high, low, m_send, m_recv, f_send, f_recv,
-              a_send, a_recv, local_sem, x_send, x_recv, send, recv, core_send, core_recv,
+              a_send, a_recv, local_sem, o_sem, x_send, x_recv, send, recv, core_send, core_recv,
               d_send, d_recv, dcore_send, dcore_recv):
     r, c, y, z, k = here()
     n_col = arrived.shape[0]
-    lead = out_ref.shape[0]
+    lead = total.shape[0]
     slab = TILE // n_col
     n = s.shape[1]
     fetch = pltpu.make_async_copy(front_ref.at[:, 0], held, local_sem.at[0])
@@ -403,7 +403,7 @@
     begin(STARTS[-2])
     arrived[0] = payload[c]
     for t in range(lead):
-        out_ref[t] = held[t * TILE:(t + 1) * TILE]
+        total[t] = held[t * TILE:(t + 1) * TILE]
     for copy in letters:
         copy.wait_recv()
 
@@ -515,14 +515,14 @@
 
             def strip(i, carry):
                 rows = pl.ds(pl.multiple_of(i * 8, 8), 8)
-                acc = [out_ref[t, rows, :] for t in range(lead)]
+                acc = [total[t, rows, :] for t in range(lead)]
                 for d, want in zip(ds, wanted):
                     part_in = arrived[d, rows, :]
                     want = jnp.broadcast_to(want, (8, TILE))
                     for t in range(lead):
                         acc[t] = acc[t] + jnp.where(want == float(t), part_in, 0.0)
                 for t in range(lead):
-                    out_ref[t, rows, :] = acc[t]
+                    total[t, rows, :] = acc[t]
                 return carry
 
             lax.fori_loop(0, TILE // 8, strip, 0)
@@ -548,7 +548,7 @@
     def _():
         at = pl.multiple_of(jnp.minimum(c, 3) * TILE, TILE)
         for t in range(lead):
-            out_ref[t] = g[:, :, :, t, :, pl.ds(at, TILE)].reshape(TILE, TILE)
+            total[t] = g[:, :, :, t, :, pl.ds(at, TILE)].reshape(TILE, TILE)
 
     @pl.when(c >= 4)
     def _():
@@ -556,7 +556,7 @@
 
         def update(t, carry):
             ah, al = split(g[:, :, :, t].reshape(TILE, n))
-            out_ref[t] = out_ref[t] - (nt(ah, high[...]) + (nt(ah, low[...]) + nt(al, high[...])))
+            total[t] = total[t] - (nt(ah, high[...]) + (nt(ah, low[...]) + nt(al, high[...])))
             return carry
 
         lax.fori_loop(1, lead, update, 0)
@@ -566,8 +566,13 @@
 
     @pl.when(c >= 4)
     def _():
-        out_ref[0] = jnp.zeros((TILE, TILE), jnp.float32)
-
+        total[0] = jnp.zeros((TILE, TILE), jnp.float32)
+
+    stores = [
+        pltpu.make_async_copy(total.at[t], out_ref.at[pl.ds(t * TILE, TILE), 0], o_sem.at[t]) for t in range(lead)
+    ]
+    for copy in stores:
+        copy.start()
     for d in range(1, n_col):
         to, copy = tile(d)
 
@@ -584,6 +589,8 @@
                         cross(h, da, mate, d).wait_send()
     for copy in letters + shares:
         copy.wait_send()
+    for copy in stores:
+        copy.wait()
 
 
 def main_call(slots, marks, mask, front, tiles):
@@ -596,10 +603,11 @@
     smem = pl.BlockSpec(memory_space=pltpu.SMEM)
     return pl.pallas_call(
         main_body,
-        out_shape=jax.ShapeDtypeStruct((lead, TILE, TILE), f32),
+        out_shape=jax.ShapeDtypeStruct(front.shape, f32),
         in_specs=[smem] * 3 + [pl.BlockSpec(memory_space=pl.ANY)] * 2,
-        out_specs=pl.BlockSpec(memory_space=pltpu.VMEM),
+        out_specs=pl.BlockSpec(memory_space=pl.ANY),
         scratch_shapes=[
+            pltpu.VMEM((lead, TILE, TILE), f32),
             pltpu.VMEM((n + lead * slab, n), f32),
             pltpu.VMEM((4, 4, 4, 2, slab, TILE), f32),
             pltpu.VMEM((4, 4, 4, 2, slab, TILE), f32),
@@ -625,6 +633,7 @@
             dma((n_col,)),
             dma((n_col,)),
             dma((3,)),
+            dma((lead,)),
             dma((2, 4, 4)),
             dma((2, 4)),
         ]

time: 202 us -> 186 us (0.921); the launches traced: 199 us -> 186 us
  Pallas kernels: 191 us -> 178 us
    pallas_call x1, Pallas kernels: 191 us -> 178 us  [main_call(): pl.pallas_call(main_body, out_shape=jax.ShapeDtypeStruct(front.shape, f32...]
    reshape x1 -> x0, local copies, waits for them, and re-layouts: 5.08 us -> none  [local(): return result.reshape(front.shape)]
    unnamed x0 -> x1, local copies, waits for them, and re-layouts: none -> 4.35 us
where the time goes in v6:
time: 186 us
  Pallas kernels  178 us (96%)
  local copies, waits for them, and re-layouts  4.35 us (2%)
  other arithmetic  2.47 us (1%)
    pallas_call x1, Pallas kernels, main_call(): pl.pallas_call(main_body, out_shape=jax.ShapeDtypeStruct(front.shape, f32...  178 us
    unnamed x1, local copies, waits for them, and re-layouts  4.35 us

profile of v6, /device:TPU:48, one launch (start us, length us, event | category | flops | bytes accessed | tf_op | source)
XLA Modules:
  0.0 185.7 jit_solution(7552965350922323306)
XLA Ops:
  0.7 0.7 add_bitcast_fusion
  1.3 1.3 select_reduce_fusion
  2.6 0.5 add_convert_fusion.mark_ref
  3.1 178.2 %shard_map.64 = f32[2048,1,256]{2,1,0:T(1,128)} custom-call(s32[32]{0:T(128)} %get-tuple-element.6.slot_ref, f32[32]{0:T(128)} %add_convert_fusion.mark_ref, s32[32]{0:T(128)} %mask_ref.1, f32[2048,1,256]{2,1,0:T(1,128)} %bitcast.12, f32[32,256,256]{2,1,0:T(8,128)} %bitcast.11), custom_call_target="tpu_custom_call" | custom-call | bytes 1000 | tf_op jit(solution)/shard_map/pallas_call | solution.py:604
  181.3 4.3 %copy.11 = f32[8,1,256,1,1,256]{5,4,3,2,1,0:T(1,128)} copy(f32[8,1,256,1,1,256]{5,4,3,2,1,0:T(1,128)} %bitcast.10) | data formatting | bytes 4194304
  (1 shorter events, 0.0 us)

commit v7 on v5

--- a/solution.py
+++ b/solution.py
@@ -230,9 +230,9 @@
 ):
     for dk in range(2):
         MOVES += [(dy, dz, dk) for dy, dz in group]
-STARTS = {-2: (1, 6), -1: (6, 10), 1: (10, 14), 3: (14, 18), 5: (18, 22)}
-EARLY = (22, 24)
-LATER = (24, 32)
+STARTS = {-2: (1, 6), -1: (6, 14), 0: (14, 18), 2: (18, 22), 4: (22, 28)}
+EARLY = (28, 28)
+LATER = (28, 32)
 
 
 def cube_gather(left, right, lower, send, recv, core_send, core_recv, r, y, z, k):
@@ -635,6 +635,28 @@
     )(slots, marks, mask, front, tiles)
 
 
+def store_body(in_ref, out_ref, sem):
+    copies = [
+        pltpu.make_async_copy(in_ref.at[t], out_ref.at[pl.ds(t * TILE, TILE), 0], sem.at[t]) for t in range(in_ref.shape[0])
+    ]
+    for copy in copies:
+        copy.start()
+    for copy in copies:
+        copy.wait()
+
+
+def store_call(x):
+    lead = x.shape[0]
+    spec = pl.BlockSpec(memory_space=pl.ANY)
+    return pl.pallas_call(
+        store_body,
+        out_shape=jax.ShapeDtypeStruct((lead * TILE, 1, TILE), x.dtype),
+        in_specs=[spec],
+        out_specs=spec,
+        scratch_shapes=[pltpu.SemaphoreType.DMA((lead,))],
+    )(x)
+
+
 def local(front, child_tiles, child_owner, child_place, child_count, tile_mask):
     n_col = lax.axis_size("col")
     lead = front.shape[0]
@@ -647,7 +669,7 @@
     slot_of = jnp.sum(jnp.where(hit, ids[None, :], 0), axis=1)
     marks = (jnp.sum(jnp.where(hit & (ids < count)[None, :], place[None, :] + 1, 0), axis=1) - 1).astype(jnp.float32)
     result = main_call(slot_of, marks, tile_mask, front.reshape(lead * TILE, 1, TILE), child_tiles.reshape(slots, TILE, TILE))
-    return result.reshape(front.shape)
+    return store_call(result).reshape(front.shape)
 
 
 def solution(mesh):

time: 202 us -> 246 us (1.22); the launches traced: 199 us -> 246 us
  Pallas kernels: 191 us -> 243 us
  local copies, waits for them, and re-layouts: 5.08 us -> 0 us
    pallas_call x0 -> x1, Pallas kernels: none -> 64.7 us  [store_call(): pl.pallas_call(store_body, out_shape=jax.ShapeDtypeStruct((lead * TILE, 1...]
    pallas_call x1, Pallas kernels: 191 us -> 178 us  [main_call(): pl.pallas_call(main_body, out_shape=jax.ShapeDtypeStruct((lead, TILE, TIL...]
    reshape x1 -> x0, local copies, waits for them, and re-layouts: 5.08 us -> none  [local(): return result.reshape(front.shape)]
where the time goes in v7:
time: 246 us
  Pallas kernels  243 us (99%)
  other arithmetic  2.47 us (1%)
    pallas_call x1, Pallas kernels, main_call(): pl.pallas_call(main_body, out_shape=jax.ShapeDtypeStruct((lead, TILE, TIL...  178 us
    pallas_call x1, Pallas kernels, store_call(): pl.pallas_call(store_body, out_shape=jax.ShapeDtypeStruct((lead * TILE, 1...  64.7 us

profile of v7, /device:TPU:48, one launch (start us, length us, event | category | flops | bytes accessed | tf_op | source)
XLA Modules:
  0.0 246.3 jit_solution(2038326790092533325)
XLA Ops:
  0.7 0.7 add_bitcast_fusion
  1.3 1.3 select_reduce_fusion
  2.6 0.5 add_convert_fusion.mark_ref
  3.1 178.3 %shard_map.64.in_ref = f32[8,256,256]{2,1,0:T(8,128)} custom-call(s32[32]{0:T(128)} %get-tuple-element.6.slot_ref, f32[32]{0:T(128)} %add_convert_fusion.mark_ref, s32[32]{0:T(128)} %mask_ref.1, f32[2048,1,256]{2,1,0:T(1,128)} %bitcast.11, f32[32,256,256]{2,1,0:T(8,128)} %bitcast.10), custom_call_target="tpu_custom_call" | custom-call | bytes 1000 | tf_op jit(solution)/shard_map/pallas_call | solution.py:597
  181.5 64.7 %shard_map.65 = f32[2048,1,256]{2,1,0:T(1,128)} custom-call(f32[8,256,256]{2,1,0:T(8,128)} %shard_map.64.in_ref), custom_call_target="tpu_custom_call" | custom-call | tf_op jit(solution)/shard_map/pallas_call | solution.py:651
  (1 shorter events, 0.0 us)

commit v8 on v7

--- a/solution.py
+++ b/solution.py
@@ -647,12 +647,11 @@
 
 def store_call(x):
     lead = x.shape[0]
-    spec = pl.BlockSpec(memory_space=pl.ANY)
     return pl.pallas_call(
         store_body,
         out_shape=jax.ShapeDtypeStruct((lead * TILE, 1, TILE), x.dtype),
-        in_specs=[spec],
-        out_specs=spec,
+        in_specs=[pl.BlockSpec(memory_space=pltpu.VMEM)],
+        out_specs=pl.BlockSpec(memory_space=pl.ANY),
         scratch_shapes=[pltpu.SemaphoreType.DMA((lead,))],
     )(x)
 

time: 246 us -> 185 us (0.75)
  Pallas kernels: 243 us -> 181 us
    pallas_call x1, Pallas kernels: 64.7 us -> 2.96 us  [store_call(): pl.pallas_call(store_body, out_shape=jax.ShapeDtypeStruct((lead * TILE, 1...]
where the time goes in v8:
time: 185 us
  Pallas kernels  181 us (98%)
  other arithmetic  2.47 us (1%)
    pallas_call x1, Pallas kernels, main_call(): pl.pallas_call(main_body, out_shape=jax.ShapeDtypeStruct((lead, TILE, TIL...  178 us

profile of v8, /device:TPU:48, one launch (start us, length us, event | category | flops | bytes accessed | tf_op | source)
XLA Modules:
  0.0 184.6 jit_solution(17733460863926262328)
XLA Ops:
  0.7 0.7 add_bitcast_fusion
  1.3 1.3 select_reduce_fusion
  2.6 0.5 add_convert_fusion.mark_ref
  3.1 178.3 %shard_map.64.in_ref = f32[8,256,256]{2,1,0:T(8,128)} custom-call(s32[32]{0:T(128)} %get-tuple-element.6.slot_ref, f32[32]{0:T(128)} %add_convert_fusion.mark_ref, s32[32]{0:T(128)} %mask_ref.1, f32[2048,1,256]{2,1,0:T(1,128)} %bitcast.11, f32[32,256,256]{2,1,0:T(8,128)} %bitcast.10), custom_call_target="tpu_custom_call" | custom-call | bytes 1000 | tf_op jit(solution)/shard_map/pallas_call | solution.py:597
  181.5 3.0 %shard_map.65 = f32[2048,1,256]{2,1,0:T(1,128)} custom-call(f32[8,256,256]{2,1,0:T(8,128)} %shard_map.64.in_ref), custom_call_target="tpu_custom_call" | custom-call | tf_op jit(solution)/shard_map/pallas_call | solution.py:650
  (1 shorter events, 0.0 us)
